TPU v7x, 32 devices: a whole 2x2x4 slice. The times are simulated.
32 devices in a mesh: parts: 2 (over x), local: 16 (over z, y, core).
Axes of the slice: x: 2, y: 2, z: 4, core: 2. Of those that a mesh axis runs over, the one named last changes fastest.
Arguments:
- rows_in: bfloat16 [512, 7168], P(('parts', 'local')), parts along dimension 0, may hold values from -6 to 6
- routes: int32 [512, 4], P(('parts', 'local')), parts along dimension 0, may hold values from 0 to 15, all different within a row; in each aligned block of 16 rows (0 to 15, 16 to 31, ...) at most 8 rows name the same one
- comb_num: int32 [512, 4], P(('parts', 'local')), parts along dimension 0, may hold values from 1 to 63
- w_gate: bfloat16 [7168, 16384], P(None, 'local'), may hold values from -0.0625 to 0.0625
- w_up: bfloat16 [7168, 16384], P(None, 'local'), may hold values from -0.0625 to 0.0625
- w_down: bfloat16 [16384, 7168], P('local'), may hold values from -0.1875 to 0.1875
Outputs:
- mixed: bfloat16 [512, 7168], P(('parts', 'local')), parts along dimension 0
There are 2 independent parts, one for each index of `parts`. A program takes and returns all parts, laid end to end along the dimension named above; an argument that names none is the same for every part. Nothing has to cross between parts.
Inputs may be any that keep to these rules, and one draw needn't show every extreme that they name: `routes`: each row names 4 different experts; among the rows of one device no expert is named by more than 8 rows, a bound that some block reaches.
All inputs are finite; a program needn't handle non-finite values.
Results may differ from a plain program's by a relative error of at most 0.0059.
Values may be sent and summed in bfloat16 or wider, within the bound.
No kernel may reach another device: no remote copies, remote signals or barrier semaphores. Data moves between devices by JAX's collectives and lax.ppermute only.
A program may use at most 128 MiB of HBM per device.

v0:
```python
import jax
import jax.numpy as jnp
from jax import lax
from jax.sharding import PartitionSpec as P

E = 16
TOP = 4
CAP = 8


denominator = 64.0


def on_device(rows_in, routes, comb_num, w_gate, w_up, w_down):
    rows_dev = rows_in.shape[0]
    feature_width = rows_in.shape[1]
    devices = lax.axis_size("local")
    split_count = devices // E
    slots = E * CAP
    flat_ids = routes.reshape(-1)
    onehot = (flat_ids[:, None] == jnp.arange(E, dtype=jnp.int32)[None, :]).astype(jnp.int32)
    slot_rank = jnp.sum((jnp.cumsum(onehot, axis=0) - 1) * onehot, axis=1)
    target = flat_ids * CAP + slot_rank
    chooser = jnp.arange(slots, dtype=jnp.int32)[:, None] == target[None, :]
    placing = jnp.sum(chooser.reshape(slots, rows_dev, TOP).astype(jnp.int32), axis=2).astype(
        jnp.bfloat16
    )
    outgoing = jnp.dot(placing, rows_in, preferred_element_type=jnp.float32).astype(jnp.bfloat16)
    weights = comb_num.reshape(-1).astype(jnp.float32) / denominator
    combine = jnp.sum(
        (chooser.T.astype(jnp.float32) * weights[:, None]).reshape(rows_dev, TOP, slots), axis=1
    )
    copies = jnp.broadcast_to(
        outgoing.reshape(E, 1, CAP, feature_width), (E, split_count, CAP, feature_width)
    ).reshape(devices, CAP, feature_width)
    items = lax.all_to_all(copies, "local", split_axis=0, concat_axis=0, tiled=True)
    shape = items.shape
    expert_items = items.reshape(-1, shape[2])
    gate_pre = jnp.dot(expert_items, w_gate, preferred_element_type=jnp.float32)
    up_pre = jnp.dot(expert_items, w_up, preferred_element_type=jnp.float32)
    hidden = (jax.nn.silu(gate_pre) * up_pre).astype(jnp.bfloat16)
    result = (
        jnp.dot(hidden, w_down, preferred_element_type=jnp.float32)
        .astype(jnp.bfloat16)
        .reshape(shape)
    )
    returned = lax.all_to_all(result, "local", split_axis=0, concat_axis=0, tiled=True)
    summed = jnp.sum(
        returned.reshape(E, split_count, CAP, feature_width).astype(jnp.float32), axis=1
    )
    summed = summed.reshape(slots, feature_width)
    mixed = jnp.dot(
        combine, summed, precision=lax.Precision.HIGHEST, preferred_element_type=jnp.float32
    )
    return mixed.astype(jnp.bfloat16)


def solution(mesh):
    in_specs = (
        P(("parts", "local"), None),
        P(("parts", "local"), None),
        P(("parts", "local"), None),
        P(None, "local"),
        P(None, "local"),
        P("local", None),
    )
    out_specs = P(("parts", "local"), None)
    return jax.shard_map(
        on_device, mesh=mesh, in_specs=in_specs, out_specs=out_specs, check_vma=False
    )
```

profile of v0, /device:TPU:15, one launch (start us, length us, event | category | flops | bytes accessed | tf_op | source)
XLA Modules:
  0.0 115.7 jit_solution(999310516775019645)
XLA Ops:
  0.0 0.0 copy-start
  0.0 0.8 copy.17
  0.8 0.1 eq.38
  0.9 0.1 fusion.13
  1.0 0.1 reduce_window_sum.11
  1.1 0.2 select_reduce_fusion.1
  1.2 0.1 reduce_sum.34
  1.3 0.1 copy.18
  1.4 0.7 multiply_add_fusion
  2.1 0.1 convert_reduce_fusion
  2.2 0.0 copy-done
  2.2 0.7 fusion
  2.9 0.0 slice-start
  2.9 48.3 %all_to_all.10 = bf16[16,8,7168]{2,1,0:T(8,128)(2,1)S(1)} all-to-all(bf16[16,8,7168]{2,1,0:T(8,128)(2,1)S(1)} %fusion), channel_id=1, replica_groups=mesh['parts'=2,'local'=16] {'local'}, dimensions={0} | all-to-all | bytes 3670016 | tf_op jit(solution)/shard_map/all_to_all | solution.py:36
  51.2 0.0 slice-start.5
  51.2 0.0 slice-start.6
  51.2 7.6 %fusion.5 = f32[128,1024]{1,0:T(8,128)S(1)} fusion(bf16[7168,1024]{1,0:T(8,128)(2,1)} %param.9, bf16[16,8,7168]{2,1,0:T(8,128)(2,1)S(1)} %all_to_all.10), kind=kOutput, calls=%fused_computation.8 | convolution fusion | flops 1879048192 | bytes 17039360 | tf_op jit(solution)/shard_map/dot_general | solution.py:39
  58.8 0.0 slice-done
  58.8 0.0 slice-done.1
  58.8 0.0 slice-done.2
  58.8 0.6 slice-done.3
  59.4 2.2 %fusion.10 = bf16[128,1024]{1,0:T(8,128)(2,1)S(1)} fusion(bf16[7168,1024]{1,0:T(8,128)(2,1)S(1)} %bitcast.23, bf16[16,8,7168]{2,1,0:T(8,128)(2,1)S(1)} %all_to_all.10, f32[128,1024]{1,0:T(8,128)S(1)} %fusion.5), kind=kOutput, calls=%fused_computation.11 | convolution fusion | flops 1879834624 | bytes 17301504 | tf_op jit(solution)/shard_map/dot_general | solution.py:40
  61.7 0.0 slice-done.4
  61.7 0.1 slice-done.5
  61.8 1.2 %slice-done.6 = s8[4194304]{0:T(1024)(128)(4,1)S(1)} async-done(((s8[14680064]{0:T(1024)(128)(4,1)}), s8[4194304]{0:T(1024)(128)(4,1)S(1)}, s32[]{:S(2)}) %slice-start.6) | async-done | bytes 4194328
  63.0 0.8 slice-done.7
  63.8 3.4 %fusion.1 = bf16[16,8,7168]{2,1,0:T(8,128)(2,1)} fusion(bf16[128,1024]{1,0:T(8,128)(2,1)S(1)} %fusion.10, bf16[1024,7168]{1,0:T(8,128)(2,1)S(1)} %bitcast.25), kind=kOutput, calls=%fused_computation.3 | convolution fusion | flops 1879965696 | bytes 16777216 | tf_op jit(solution)/shard_map/dot_general | solution.py:43
  67.2 5.2 %all-to-all-start.1 = ((bf16[16,8,7168]{2,1,0:T(8,128)(2,1)}), bf16[16,8,7168]{2,1,0:T(8,128)(2,1)S(1)}, u32[]{:S(2)}, u32[]{:S(2)}) async-start(bf16[16,8,7168]{2,1,0:T(8,128)(2,1)} %fusion.1), calls=%async_computation.1 | async-start | bytes 3670016 | tf_op jit(solution)/shard_map/all_to_all | solution.py:47
  72.4 0.0 copy-done.1
  72.4 0.1 select_reduce_fusion
  72.5 41.7 %all-to-all-done.1 = bf16[16,8,7168]{2,1,0:T(8,128)(2,1)S(1)} async-done(((bf16[16,8,7168]{2,1,0:T(8,128)(2,1)}), bf16[16,8,7168]{2,1,0:T(8,128)(2,1)S(1)}, u32[]{:S(2)}, u32[]{:S(2)}) %all-to-all-start.1) | async-done | bytes 1835040 | tf_op jit(solution)/shard_map/all_to_all | solution.py:47
  114.2 1.5 %convolution_convert_fusion.2 = bf16[16,7168]{1,0:T(8,128)(2,1)} fusion(f32[16,128]{1,0:T(8,128)S(1)} %select_reduce_fusion, bf16[16,8,7168]{2,1,0:T(8,128)(2,1)S(1)} %all-to-all-done.1), kind=kOutput, calls=%fused_computation.4 | convolution fusion | flops 176275456 | bytes 2072576 | tf_op jit(solution)/shard_map/dot_general | solution.py:52
  (9 shorter events, 0.0 us)
Async XLA Ops:
  0.0 2.2 %copy-start = (bf16[16,7168]{1,0:T(8,128)(2,1)S(1)}, bf16[16,7168]{1,0:T(8,128)(2,1)}, u32[]{:S(2)}) copy-start(bf16[16,7168]{1,0:T(8,128)(2,1)} %param.6) | copy-start | bytes 688132
  2.9 55.9 %slice-start = ((s8[14680064]{0:T(1024)(128)(4,1)}), s8[4194304]{0:T(1024)(128)(4,1)S(1)}, s32[]{:S(2)}) async-start(s8[14680064]{0:T(1024)(128)(4,1)} %bitcast.22), calls=%async_computation.2 | async-start | bytes 8388608
  51.2 7.6 %slice-start.1 = ((s8[14680064]{0:T(1024)(128)(4,1)}), s8[4194304]{0:T(1024)(128)(4,1)S(1)}, s32[]{:S(2)}) async-start(s8[14680064]{0:T(1024)(128)(4,1)} %bitcast.22), calls=%async_computation.3 | async-start | bytes 8388608
  51.2 7.6 %slice-start.2 = ((s8[14680064]{0:T(1024)(128)(4,1)}), s8[4194304]{0:T(1024)(128)(4,1)S(1)}, s32[]{:S(2)}) async-start(s8[14680064]{0:T(1024)(128)(4,1)} %bitcast.22), calls=%async_computation.4 | async-start | bytes 8388608
  51.2 8.2 %slice-start.3 = ((s8[14680064]{0:T(1024)(128)(4,1)}), s8[2097152]{0:T(1024)(128)(4,1)S(1)}, s32[]{:S(2)}) async-start(s8[14680064]{0:T(1024)(128)(4,1)} %bitcast.22), calls=%async_computation.5 | async-start | bytes 4194304
  51.2 10.5 %slice-start.4 = ((s8[14680064]{0:T(1024)(128)(4,1)}), s8[4194304]{0:T(1024)(128)(4,1)S(1)}, s32[]{:S(2)}) async-start(s8[14680064]{0:T(1024)(128)(4,1)} %bitcast.24), calls=%async_computation.6 | async-start | bytes 8388608
  51.2 10.6 %slice-start.5 = ((s8[14680064]{0:T(1024)(128)(4,1)}), s8[4194304]{0:T(1024)(128)(4,1)S(1)}, s32[]{:S(2)}) async-start(s8[14680064]{0:T(1024)(128)(4,1)} %bitcast.24), calls=%async_computation.7 | async-start | bytes 8388608
  51.2 11.8 %slice-start.6 = ((s8[14680064]{0:T(1024)(128)(4,1)}), s8[4194304]{0:T(1024)(128)(4,1)S(1)}, s32[]{:S(2)}) async-start(s8[14680064]{0:T(1024)(128)(4,1)} %bitcast.24), calls=%async_computation.8 | async-start | bytes 8388608
  59.4 4.4 %slice-start.7 = ((s8[14680064]{0:T(1024)(128)(4,1)}), s8[2097152]{0:T(1024)(128)(4,1)S(1)}, s32[]{:S(2)}) async-start(s8[14680064]{0:T(1024)(128)(4,1)} %bitcast.24), calls=%async_computation.9 | async-start | bytes 4194304
  67.2 5.2 %copy-start.1 = (s32[16,4]{0,1:T(4,128)S(1)}, s32[16,4]{0,1:T(4,128)}, u32[]{:S(2)}) copy-start(s32[16,4]{0,1:T(4,128)} %param.8) | copy-start | bytes 772
  67.2 47.0 %all-to-all-start.1 = ((bf16[16,8,7168]{2,1,0:T(8,128)(2,1)}), bf16[16,8,7168]{2,1,0:T(8,128)(2,1)S(1)}, u32[]{:S(2)}, u32[]{:S(2)}) async-start(bf16[16,8,7168]{2,1,0:T(8,128)(2,1)} %fusion.1), calls=%async_computation.1 | async-start | bytes 3670016 | tf_op jit(solution)/shard_map/all_to_all | solution.py:47
where the time goes:
time: 116 us
  blocking collectives  48.3 us (42%)
  waiting for transfers between devices  41.7 us (36%)
  matrix products  15.3 us (13%)
  starting transfers between devices  5.22 us (4%)
  local copies, waits for them, and re-layouts  3.86 us (3%)
  other arithmetic  1.21 us (1%)
    all_to_all x1, blocking collectives, on_device(): lax.all_to_all(copies, 'local', split_axis=0, concat_axis=0, tiled=True)  48.3 us
    all_to_all x1, waiting for transfers between devices, on_device(): lax.all_to_all(result, 'local', split_axis=0, concat_axis=0, tiled=True)  41.7 us
    dot_general x1, matrix products, on_device(): gate_pre = jnp.dot(expert_items, w_gate, preferred_element_type=jnp.float32)  7.55 us
    all_to_all x1, starting transfers between devices, on_device(): lax.all_to_all(result, 'local', split_axis=0, concat_axis=0, tiled=True)  5.22 us
    unnamed x21, local copies, waits for them, and re-layouts  3.6 us
    dot_general x1, matrix products, on_device(): jnp.dot(hidden, w_down, preferred_element_type=jnp.float32)  3.36 us
  transfers between devices with their start and end apart: 1, of which 1 were waited for; matrix products, arithmetic and copies ran while one was open for 0% of the time, Pallas kernels for 0%

commit v1 on v0

v1 whole, which is shorter than its diff:
```python
import functools

import jax
import jax.numpy as jnp
from jax import lax
from jax.experimental import pallas as pl
from jax.experimental.pallas import tpu as pltpu
from jax.sharding import PartitionSpec as P

E = 16
CAP = 8
LANES = 128
AHEAD = 5
denominator = 64.0
VMEM = pl.BlockSpec(memory_space=pltpu.VMEM)
SMEM = pl.BlockSpec(memory_space=pltpu.SMEM)
ANY = pl.BlockSpec(memory_space=pl.ANY)
HBM = pl.BlockSpec(memory_space=pltpu.HBM)


def exchange(x, distance):
    n = lax.axis_size("local")
    return lax.ppermute(x, "local", [(i, i ^ distance) for i in range(n)])


def pack_kernel(rows_ref, routes_ref, comb_ref, out_ref):
    rows, width = rows_ref.shape
    out_ref[:, :width] = rows_ref[...]
    sub = lax.broadcasted_iota(jnp.int32, (LANES, rows), 0)
    table = jnp.zeros((LANES, rows), jnp.int32)
    for k in range(routes_ref.shape[0]):
        table = jnp.where(sub == routes_ref[k : k + 1, :], comb_ref[k : k + 1, :], table)
    same = lax.broadcasted_iota(jnp.int32, (rows, rows), 0) == lax.broadcasted_iota(jnp.int32, (rows, rows), 1)
    turned = lax.dot_general(
        same.astype(jnp.float32).astype(jnp.bfloat16),
        table.astype(jnp.float32).astype(jnp.bfloat16),
        (((1,), (1,)), ((), ())), preferred_element_type=jnp.float32,
    )
    out_ref[:, width:] = turned.astype(jnp.bfloat16)


def pack(rows, routes, comb):
    return pl.pallas_call(
        pack_kernel,
        out_shape=jax.ShapeDtypeStruct((rows.shape[0], rows.shape[1] + LANES), rows.dtype),
        in_specs=[VMEM] * 3,
        out_specs=VMEM,
        name="pack",
    )(rows, routes.T, comb.T)


def tile_of(width, most):
    return max(t for t in range(LANES, most + 1, LANES) if width % t == 0)


def advance(copies, i):
    copies[i].wait()
    if i + AHEAD < len(copies):
        copies[i + AHEAD].start()


def expert_kernel(blocks, expert_ref, *refs):
    block_refs, refs = refs[:blocks], refs[blocks:]
    gate_hbm, up_hbm, down_hbm, refs = refs[0], refs[1], refs[2], refs[3:]
    keep_out, send_out, hidden_ref, combine_ref, refs = *refs[:4], refs[4:]
    rows_ref, gate_ref, up_ref, down_ref, gate_sum, up_sum, sems, weight_sems = refs
    count, total = rows_ref.shape
    width = total - LANES
    block = count // blocks
    slots = hidden_ref.shape[0]
    deep = tile_of(width, 1024)
    steps = width // deep

    copies = [
        pltpu.make_async_copy(ref, rows_ref.at[pl.ds(i * block, block), :], sems.at[i])
        for i, ref in enumerate(block_refs)
    ]
    near = []
    for j in range(steps):
        c = pl.ds(j * deep, deep)
        near.append(pltpu.make_async_copy(gate_hbm.at[c, :], gate_ref.at[c, :], weight_sems.at[2 * j]))
        near.append(pltpu.make_async_copy(up_hbm.at[c, :], up_ref.at[c, :], weight_sems.at[2 * j + 1]))
    for j in range(steps):
        c = pl.ds(j * deep, deep)
        near.append(
            pltpu.make_async_copy(down_hbm.at[:, c], down_ref.at[:, c], weight_sems.at[2 * steps + j])
        )
    for copy in copies + near[:AHEAD]:
        copy.start()
    for copy in copies:
        copy.wait()

    table = rows_ref[:, width:]
    mine = (lax.broadcasted_iota(jnp.int32, (8, LANES), 1) == expert_ref[0]).astype(jnp.float32)
    along = lax.dot_general(
        mine.astype(jnp.bfloat16), table, (((1,), (1,)), ((), ())),
        preferred_element_type=jnp.float32,
    )
    down_col = jnp.sum(table.astype(jnp.float32) * mine[:1, :], axis=1, keepdims=True)
    r = lax.broadcasted_iota(jnp.int32, (count, count), 0)
    s = lax.broadcasted_iota(jnp.int32, (count, count), 1)
    same = (r // block) == (s // block)
    before = (same & (r < s)).astype(jnp.float32).astype(jnp.bfloat16)
    after = (same & (s < r)).astype(jnp.float32).astype(jnp.bfloat16)
    chosen = (along > 0).astype(jnp.float32)
    rank = jnp.dot(chosen.astype(jnp.bfloat16), before, preferred_element_type=jnp.float32)
    start = (lax.broadcasted_iota(jnp.int32, (8, count), 1) // block) * CAP
    slot = jnp.where(along > 0, rank.astype(jnp.int32) + start, slots)[:1, :]
    place = (lax.broadcasted_iota(jnp.int32, (slots, count), 0) == slot)
    place = place.astype(jnp.float32).astype(jnp.bfloat16)
    chosen_col = jnp.broadcast_to((down_col > 0).astype(jnp.float32), (count, LANES))
    rank_col = jnp.dot(after, chosen_col.astype(jnp.bfloat16), preferred_element_type=jnp.float32)
    start_col = (lax.broadcasted_iota(jnp.int32, (count, 1), 0) // block) * CAP
    slot_col = rank_col[:, :1].astype(jnp.int32) + start_col
    combine = jnp.where(
        lax.broadcasted_iota(jnp.int32, (count, slots), 1) == slot_col,
        down_col / denominator, 0.0,
    ).astype(jnp.bfloat16)

    combine_ref[...] = combine

    for j in range(steps):
        c = pl.ds(j * deep, deep)
        items = jnp.dot(place, rows_ref[:, c], preferred_element_type=jnp.float32)
        items = items.astype(jnp.bfloat16)
        advance(near, 2 * j)
        gate = jnp.dot(items, gate_ref[c, :], preferred_element_type=jnp.float32)
        advance(near, 2 * j + 1)
        up = jnp.dot(items, up_ref[c, :], preferred_element_type=jnp.float32)
        if j > 0:
            gate, up = gate_sum[...] + gate, up_sum[...] + up
        gate_sum[...], up_sum[...] = gate, up
    gate = gate_sum[...]
    hidden_ref[...] = (gate / (1.0 + jnp.exp(-gate)) * up_sum[...]).astype(jnp.bfloat16)

    spread(
        hidden_ref, combine_ref, 0, down_ref, near, 2 * steps, deep, (keep_out, send_out)
    )


def spread(hidden_ref, combine_ref, first, down_ref, copies, passed, deep, outs):
    count = sum(out.shape[0] for out in outs)
    for j in range(len(copies) - passed):
        advance(copies, passed + j)
        c = pl.ds(j * deep, deep)
        piece = jnp.dot(
            hidden_ref[...], down_ref[:, c], preferred_element_type=jnp.float32
        ).astype(jnp.bfloat16)
        part = jnp.dot(
            combine_ref[first : first + count, :], piece, preferred_element_type=jnp.float32
        ).astype(jnp.bfloat16)
        start = 0
        for out in outs:
            out[:, c] = part[start : start + out.shape[0], :]
            start += out.shape[0]


def rest_kernel(first, hidden_ref, combine_ref, down_hbm, after_ref, *refs):
    outs, down_ref, sems = refs[:-2], refs[-2], refs[-1]
    steps = sems.shape[0]
    deep = down_ref.shape[1] // steps
    copies = [
        pltpu.make_async_copy(
            down_hbm.at[:, pl.ds(j * deep, deep)], down_ref.at[:, pl.ds(j * deep, deep)], sems.at[j]
        )
        for j in range(steps)
    ]
    for copy in copies[:AHEAD]:
        copy.start()
    spread(hidden_ref, combine_ref, first, down_ref, copies, 0, deep, outs)


def expert_rest(hidden, combine, w_down, after, first, pieces):
    width = w_down.shape[1]
    return pl.pallas_call(
        functools.partial(rest_kernel, first),
        out_shape=[jax.ShapeDtypeStruct((rows, width), jnp.bfloat16) for rows in pieces],
        in_specs=[VMEM, VMEM, HBM, ANY],
        out_specs=[VMEM] * len(pieces),
        scratch_shapes=[
            pltpu.VMEM(w_down.shape, jnp.bfloat16),
            pltpu.SemaphoreType.DMA((width // tile_of(width, 1024),)),
        ],
        compiler_params=pltpu.CompilerParams(vmem_limit_bytes=48 << 20),
        cost_estimate=pl.CostEstimate(
            flops=4 * hidden.shape[0] * w_down.size, bytes_accessed=w_down.size * 2, transcendentals=0
        ),
        name="rest",
    )(hidden, combine, pltpu.with_memory_space_constraint(w_down, pltpu.HBM), after)


def expert_part(expert, blocks, w_gate, w_up, w_down, piece):
    n = len(blocks)
    block, total = blocks[0].shape
    width = total - LANES
    units = w_gate.shape[1]
    count = n * block
    slots = n * CAP
    flops = 2 * slots * units * width * 3
    weights = [pltpu.with_memory_space_constraint(w, pltpu.HBM) for w in (w_gate, w_up, w_down)]
    return pl.pallas_call(
        functools.partial(expert_kernel, n),
        out_shape=[
            jax.ShapeDtypeStruct((piece, width), jnp.bfloat16),
            jax.ShapeDtypeStruct((piece, width), jnp.bfloat16),
            jax.ShapeDtypeStruct((slots, units), jnp.bfloat16),
            jax.ShapeDtypeStruct((count, slots), jnp.bfloat16),
        ],
        in_specs=[SMEM] + [ANY] * n + [HBM] * 3,
        out_specs=[VMEM] * 4,
        scratch_shapes=[
            pltpu.VMEM((count, total), jnp.bfloat16),
            pltpu.VMEM(w_gate.shape, jnp.bfloat16),
            pltpu.VMEM(w_up.shape, jnp.bfloat16),
            pltpu.VMEM(w_down.shape, jnp.bfloat16),
            pltpu.VMEM((slots, units), jnp.float32),
            pltpu.VMEM((slots, units), jnp.float32),
            pltpu.SemaphoreType.DMA((n,)),
            pltpu.SemaphoreType.DMA((3 * width // tile_of(width, 1024),)),
        ],
        compiler_params=pltpu.CompilerParams(vmem_limit_bytes=58 << 20),
        cost_estimate=pl.CostEstimate(
            flops=flops, bytes_accessed=w_down.size * 6, transcendentals=0
        ),
        name="expert",
    )(expert, *blocks, *weights)


def add(a, b, after=None):
    total = a.astype(jnp.float32) + b.astype(jnp.float32)
    if after is not None:
        total = total + after[0, 0].astype(jnp.float32) * 0.0
    return total.astype(jnp.bfloat16)


def on_device(rows_in, routes, comb_num, w_gate, w_up, w_down):
    n = lax.axis_size("local")
    me = lax.axis_index("local")
    b = rows_in.shape[0]
    expert = (me // (n // E)).astype(jnp.int32).reshape(1)
    far = range(n - 4, 4, -4)

    own = pack(rows_in, routes, comb_num)
    got = {0: own}
    got[n - 4] = exchange(own, n - 4)
    got[2] = exchange(own, 2)
    got[4] = exchange(own, 4)
    got[1] = exchange(own, 1)
    got[6] = exchange(got[2], 4)
    for k in far[1:]:
        got[k] = exchange(own, k)
    for k in far:
        got[k | 2] = exchange(got[k], 2)
    for k in range(2, n, 2):
        got[k | 1] = exchange(got[k], 1)

    first = n - 4
    planes = [*far, 4, 0]
    order = [k | i for k in planes for i in (0, 2, 1, 3)]
    keep, send, hidden, combine = expert_part(
        expert, [got[k] for k in order], w_gate, w_up, w_down, 2 * b
    )
    both = {first: add(keep, exchange(send, 1))}
    parts = expert_rest(hidden, combine, w_down, both[first], 4 * b, (2 * b,) * (n // 2 - 2))
    last = both[first]
    for i, k in enumerate(planes[1:]):
        last = both[k] = add(parts[2 * i], exchange(parts[2 * i + 1], 1), last)
    last = None
    came = []
    for k in planes:
        last = add(both[k][:b], exchange(both[k][b:], 2), last)
        came.append(exchange(last, k) if k else last)
    total = came[0].astype(jnp.float32)
    for piece in came[1:]:
        total = total + piece.astype(jnp.float32)
    return total.astype(jnp.bfloat16)


def solution(mesh):
    in_specs = (
        P(("parts", "local"), None),
        P(("parts", "local"), None),
        P(("parts", "local"), None),
        P(None, "local"),
        P(None, "local"),
        P("local", None),
    )
    out_specs = P(("parts", "local"), None)
    return jax.shard_map(
        on_device, mesh=mesh, in_specs=in_specs, out_specs=out_specs, check_vma=False
    )
```

time: 116 us -> 102 us (0.88)
  the two profiles are of different devices: /device:TPU:15 before, /device:TPU:0 now
where the time goes in v1:
time: 102 us
  waiting for transfers between devices  41.6 us (41%)
  Pallas kernels  25.9 us (25%)
  starting transfers between devices  21.9 us (21%)
  local copies, waits for them, and re-layouts  5.63 us (6%)
  between operations  4.27 us (4%)
  other arithmetic  2.58 us (3%)
    ppermute x26, waiting for transfers between devices, exchange(): return lax.ppermute(x, 'local', [(i, i ^ distance) for i in range(n)])  41.6 us
    ppermute x26, starting transfers between devices, exchange(): return lax.ppermute(x, 'local', [(i, i ^ distance) for i in range(n)])  21.9 us
    pallas_call x1, Pallas kernels, expert_part(): pl.pallas_call(functools.partial(expert_kernel, n), out_shape=[jax.ShapeD...  17.9 us
    pallas_call x1, Pallas kernels, expert_rest(): pl.pallas_call(functools.partial(rest_kernel, first), out_shape=[jax.Shap...  6.26 us
    slice x6, local copies, waits for them, and re-layouts, add(): total = total + after[0, 0].astype(jnp.float32) * 0.0  3.15 us
    unnamed x34, local copies, waits for them, and re-layouts  2.41 us
  transfers between devices with their start and end apart: 26, of which 12 were waited for; matrix products, arithmetic and copies ran while one was open for 3% of the time, Pallas kernels for 6%

profile of v1, /device:TPU:0, one launch (start us, length us, event | category | flops | bytes accessed | tf_op | source)
XLA Modules:
  0.0 101.9 jit_solution(14477840578489496124)
XLA Ops:
  0.0 1.8 %pack.1.refs_12_ = bf16[16,7296]{1,0:T(8,128)(2,1)} custom-call(bf16[16,7168]{1,0:T(8,128)(2,1)} %rows_ref.1, s32[4,16]{1,0:T(4,128)} %bitcast.9, s32[4,16]{1,0:T(4,128)} %bitcast.10), custom_call_target="tpu_custom_call" | custom-call | tf_op jit(solution)/shard_map/pack/pallas_call | solution.py:43
  1.8 3.0 %collective-permute-start.9 = (bf16[16,7296]{1,0:T(8,128)(2,1)}, bf16[16,7296]{1,0:T(8,128)(2,1)S(1)}, u32[]{:S(2)}, u32[]{:S(2)}) collective-permute-start(bf16[16,7296]{1,0:T(8,128)(2,1)} %pack.1.refs_12_), channel_id=1, source_target_pairs={{0,2},{1,3},{2,0},{3,1},{4,6},{5,7},{6,4},{7,5},{8,10},{9,11},{10,... | collective-permute-start | bytes 700424 | tf_op jit(solution)/shard_map/ppermute | solution.py:23
  4.8 1.6 %collective-permute-start.8 = (bf16[16,7296]{1,0:T(8,128)(2,1)}, bf16[16,7296]{1,0:T(8,128)(2,1)S(1)}, u32[]{:S(2)}, u32[]{:S(2)}) collective-permute-start(bf16[16,7296]{1,0:T(8,128)(2,1)} %pack.1.refs_12_), channel_id=1, source_target_pairs={{0,4},{1,5},{2,6},{3,7},{4,0},{5,1},{6,2},{7,3},{8,12},{9,13},{10,... | collective-permute-start | bytes 700424 | tf_op jit(solution)/shard_map/ppermute | solution.py:23
  6.3 2.6 %collective-permute-start.4 = (bf16[16,7296]{1,0:T(8,128)(2,1)}, bf16[16,7296]{1,0:T(8,128)(2,1)S(1)}, u32[]{:S(2)}, u32[]{:S(2)}) collective-permute-start(bf16[16,7296]{1,0:T(8,128)(2,1)} %pack.1.refs_12_), channel_id=1, source_target_pairs={{0,8},{1,9},{2,10},{3,11},{4,12},{5,13},{6,14},{7,15},{8,0},{9,1},... | collective-permute-start | bytes 700424 | tf_op jit(solution)/shard_map/ppermute | solution.py:23
  9.2 1.5 %collective-permute-done.9.refs_13_ = bf16[16,7296]{1,0:T(8,128)(2,1)S(1)} collective-permute-done((bf16[16,7296]{1,0:T(8,128)(2,1)}, bf16[16,7296]{1,0:T(8,128)(2,1)S(1)}, u32[]{:S(2)}, u32[]{:S(2)}) %collective-permute-start.9) | collective-permute-done | bytes 233504 | tf_op jit(solution)/shard_map/ppermute | solution.py:23
  10.7 1.9 %collective-permute-start.10 = (bf16[16,7296]{1,0:T(8,128)(2,1)S(1)}, bf16[16,7296]{1,0:T(8,128)(2,1)S(1)}, u32[]{:S(2)}, u32[]{:S(2)}) collective-permute-start(bf16[16,7296]{1,0:T(8,128)(2,1)S(1)} %collective-permute-done.9.refs_13_), channel_id=1, source_target_pairs={{0,4},{1,5},{2,6},{3,7},{4,0},{5,1},{6,2},{7,3},{8,12},{9,13},{10,... | collective-permute-start | bytes 700424 | tf_op jit(solution)/shard_map/ppermute | solution.py:23
  12.6 5.5 %collective-permute-done.8.refs_8_ = bf16[16,7296]{1,0:T(8,128)(2,1)S(1)} collective-permute-done((bf16[16,7296]{1,0:T(8,128)(2,1)}, bf16[16,7296]{1,0:T(8,128)(2,1)S(1)}, u32[]{:S(2)}, u32[]{:S(2)}) %collective-permute-start.8) | collective-permute-done | bytes 233504 | tf_op jit(solution)/shard_map/ppermute | solution.py:23
  18.1 8.0 %collective-permute-done.4.refs_4_ = bf16[16,7296]{1,0:T(8,128)(2,1)S(1)} collective-permute-done((bf16[16,7296]{1,0:T(8,128)(2,1)}, bf16[16,7296]{1,0:T(8,128)(2,1)S(1)}, u32[]{:S(2)}, u32[]{:S(2)}) %collective-permute-start.4) | collective-permute-done | bytes 233504 | tf_op jit(solution)/shard_map/ppermute | solution.py:23
  26.6 1.5 %collective-permute-start.1 = (bf16[16,7296]{1,0:T(8,128)(2,1)S(1)}, bf16[16,7296]{1,0:T(8,128)(2,1)S(1)}, u32[]{:S(2)}, u32[]{:S(2)}) collective-permute-start(bf16[16,7296]{1,0:T(8,128)(2,1)S(1)} %collective-permute-done.refs_0_), channel_id=1, source_target_pairs={{0,2},{1,3},{2,0},{3,1},{4,6},{5,7},{6,4},{7,5},{8,10},{9,11},{10,... | collective-permute-start | bytes 700424 | tf_op jit(solution)/shard_map/ppermute | solution.py:23
  28.7 3.8 %collective-permute-done.5.refs_5_ = bf16[16,7296]{1,0:T(8,128)(2,1)S(1)} collective-permute-done((bf16[16,7296]{1,0:T(8,128)(2,1)S(1)}, bf16[16,7296]{1,0:T(8,128)(2,1)S(1)}, u32[]{:S(2)}, u32[]{:S(2)}) %collective-permute-start.5) | collective-permute-done | bytes 233504 | tf_op jit(solution)/shard_map/ppermute | solution.py:23
  32.5 2.5 %collective-permute-done.1.refs_1_ = bf16[16,7296]{1,0:T(8,128)(2,1)S(1)} collective-permute-done((bf16[16,7296]{1,0:T(8,128)(2,1)S(1)}, bf16[16,7296]{1,0:T(8,128)(2,1)S(1)}, u32[]{:S(2)}, u32[]{:S(2)}) %collective-permute-start.1) | collective-permute-done | bytes 233504 | tf_op jit(solution)/shard_map/ppermute | solution.py:23
  35.1 1.4 %collective-permute-done.3.refs_3_ = bf16[16,7296]{1,0:T(8,128)(2,1)S(1)} collective-permute-done((bf16[16,7296]{1,0:T(8,128)(2,1)S(1)}, bf16[16,7296]{1,0:T(8,128)(2,1)S(1)}, u32[]{:S(2)}, u32[]{:S(2)}) %collective-permute-start.3) | collective-permute-done | bytes 233504 | tf_op jit(solution)/shard_map/ppermute | solution.py:23
  36.7 0.6 copy-done.16
  37.2 17.9 %expert.1 = (bf16[32,7168]{1,0:T(8,128)(2,1)}, bf16[32,7168]{1,0:T(8,128)(2,1)}, bf16[128,1024]{1,0:T(8,128)(2,1)}, bf16[256,128]{1,0:T(8,128)(2,1)}) custom-call(s32[1]{0:T(128)} %bitcast.expert_ref, bf16[16,7296]{1,0:T(8,128)(2,1)} %copy-done.6, bf16[16,7296]{1,0:T(8,128)(2,1)} %copy-done.11, bf16[16,7296]{1,0:T(8,128)(2,1)} %copy-done.13, ...), custom_call_target="tpu_custom_call" | custom-call | flops 5637144576 | bytes 44040192 | tf_op jit(solution)/shard_map/expert/pallas_call | solution.py:201
  55.3 1.9 %collective-permute-done.15 = bf16[32,7168]{1,0:T(8,128)(2,1)S(1)} collective-permute-done((bf16[32,7168]{1,0:T(8,128)(2,1)}, bf16[32,7168]{1,0:T(8,128)(2,1)S(1)}, u32[]{:S(2)}, u32[]{:S(2)}) %collective-permute-start.15) | collective-permute-done | bytes 458784 | tf_op jit(solution)/shard_map/ppermute | solution.py:23
  57.2 1.1 %add_convert_fusion.3.after_ref = bf16[32,7168]{1,0:T(8,128)(2,1)S(1)} fusion(bf16[32,7168]{1,0:T(8,128)(2,1)S(1)} %collective-permute-done.15, bf16[32,7168]{1,0:T(8,128)(2,1)} %get-tuple-element.15), kind=kLoop, calls=%fused_computation.3 | loop fusion | flops 917504 | bytes 1376256 | tf_op jit(solution)/shard_map/convert_element_type | solution.py:233
  58.3 0.5 slice.58
  58.9 0.6 collective-permute-start.16
  59.4 0.9 copy-done
  60.4 0.8 copy-done.1
  61.2 6.3 %rest.1 = (bf16[32,7168]{1,0:T(8,128)(2,1)S(1)}, bf16[32,7168]{1,0:T(8,128)(2,1)S(1)}, bf16[32,7168]{1,0:T(8,128)(2,1)S(1)}, bf16[32,7168]{1,0:T(8,128)(2,1)S(1)...) custom-call(bf16[128,1024]{1,0:T(8,128)(2,1)S(1)} %copy-done, bf16[256,128]{1,0:T(8,128)(2,1)S(1)} %copy-done.1, ...), custom_call_target="tpu_custom_call" | custom-call | flops 3758096384 | bytes 14680064 | tf_op jit(solution)/shard_map/rest/pallas_call | solution.py:175
  68.8 0.6 slice.61
  69.4 4.8 %collective-permute-start.17 = (bf16[16,7168]{1,0:T(8,128)(2,1)S(1)}, bf16[16,7168]{1,0:T(8,128)(2,1)S(1)}, u32[]{:S(2)}, u32[]{:S(2)}) collective-permute-start(bf16[16,7168]{1,0:T(8,128)(2,1)S(1)} %add_convert_fusion.8), channel_id=1, source_target_pairs={{0,12},{1,13},{2,14},{3,15},{4,8},{5,9},{6,10},{7,11},{8,4},{9,5},... | collective-permute-start | bytes 688136 | tf_op jit(solution)/shard_map/ppermute | solution.py:23
  77.0 1.6 %collective-permute-start.19 = (bf16[16,7168]{1,0:T(8,128)(2,1)S(1)}, bf16[16,7168]{1,0:T(8,128)(2,1)S(1)}, u32[]{:S(2)}, u32[]{:S(2)}) collective-permute-start(bf16[16,7168]{1,0:T(8,128)(2,1)S(1)} %slice.60), channel_id=1, source_target_pairs={{0,2},{1,3},{2,0},{3,1},{4,6},{5,7},{6,4},{7,5},{8,10},{9,11},{10,... | collective-permute-start | bytes 688136 | tf_op jit(solution)/shard_map/ppermute | solution.py:23
  79.2 0.6 collective-permute-start.22
  80.0 1.6 %collective-permute-start.25 = (bf16[16,7168]{1,0:T(8,128)(2,1)S(1)}, bf16[16,7168]{1,0:T(8,128)(2,1)S(1)}, u32[]{:S(2)}, u32[]{:S(2)}) collective-permute-start(bf16[16,7168]{1,0:T(8,128)(2,1)S(1)} %slice.68), channel_id=1, source_target_pairs={{0,2},{1,3},{2,0},{3,1},{4,6},{5,7},{6,4},{7,5},{8,10},{9,11},{10,... | collective-permute-start | bytes 688136 | tf_op jit(solution)/shard_map/ppermute | solution.py:23
  81.5 4.0 %collective-permute-done.19 = bf16[16,7168]{1,0:T(8,128)(2,1)S(1)} collective-permute-done((bf16[16,7168]{1,0:T(8,128)(2,1)S(1)}, bf16[16,7168]{1,0:T(8,128)(2,1)S(1)}, u32[]{:S(2)}, u32[]{:S(2)}) %collective-permute-start.19) | collective-permute-done | bytes 229408 | tf_op jit(solution)/shard_map/ppermute | solution.py:23
  86.7 3.7 %collective-permute-done.22 = bf16[16,7168]{1,0:T(8,128)(2,1)S(1)} collective-permute-done((bf16[16,7168]{1,0:T(8,128)(2,1)S(1)}, bf16[16,7168]{1,0:T(8,128)(2,1)S(1)}, u32[]{:S(2)}, u32[]{:S(2)}) %collective-permute-start.22) | collective-permute-done | bytes 229408 | tf_op jit(solution)/shard_map/ppermute | solution.py:23
  91.7 2.8 %collective-permute-done.25 = bf16[16,7168]{1,0:T(8,128)(2,1)S(1)} collective-permute-done((bf16[16,7168]{1,0:T(8,128)(2,1)S(1)}, bf16[16,7168]{1,0:T(8,128)(2,1)S(1)}, u32[]{:S(2)}, u32[]{:S(2)}) %collective-permute-start.25) | collective-permute-done | bytes 229408 | tf_op jit(solution)/shard_map/ppermute | solution.py:23
  94.5 2.6 %collective-permute-done.20 = bf16[16,7168]{1,0:T(8,128)(2,1)S(1)} collective-permute-done((bf16[16,7168]{1,0:T(8,128)(2,1)S(1)}, bf16[16,7168]{1,0:T(8,128)(2,1)S(1)}, u32[]{:S(2)}, u32[]{:S(2)}) %collective-permute-start.20) | collective-permute-done | bytes 229408 | tf_op jit(solution)/shard_map/ppermute | solution.py:23
  97.2 3.8 %collective-permute-done.23 = bf16[16,7168]{1,0:T(8,128)(2,1)S(1)} collective-permute-done((bf16[16,7168]{1,0:T(8,128)(2,1)S(1)}, bf16[16,7168]{1,0:T(8,128)(2,1)S(1)}, u32[]{:S(2)}, u32[]{:S(2)}) %collective-permute-start.23) | collective-permute-done | bytes 229408 | tf_op jit(solution)/shard_map/ppermute | solution.py:23
  101.0 0.8 add_convert_fusion.4
  (75 shorter events, 5.1 us)
Async XLA Ops:
  1.8 8.9 %collective-permute-start.9 = (bf16[16,7296]{1,0:T(8,128)(2,1)}, bf16[16,7296]{1,0:T(8,128)(2,1)S(1)}, u32[]{:S(2)}, u32[]{:S(2)}) collective-permute-start(bf16[16,7296]{1,0:T(8,128)(2,1)} %pack.1.refs_12_), channel_id=1, source_target_pairs={{0,2},{1,3},{2,0},{3,1},{4,6},{5,7},{6,4},{7,5},{8,10},{9,11},{10,... | collective-permute-start | bytes 700424 | tf_op jit(solution)/shard_map/ppermute | solution.py:23
  4.8 5.9 %collective-permute-start.13 = (bf16[16,7296]{1,0:T(8,128)(2,1)}, bf16[16,7296]{1,0:T(8,128)(2,1)S(1)}, u32[]{:S(2)}, u32[]{:S(2)}) collective-permute-start(bf16[16,7296]{1,0:T(8,128)(2,1)} %pack.1.refs_12_), channel_id=1, source_target_pairs={{0,1},{1,0},{2,3},{3,2},{4,5},{5,4},{6,7},{7,6},{8,9},{9,8},{10,11... | collective-permute-start | bytes 700424 | tf_op jit(solution)/shard_map/ppermute | solution.py:23
  4.8 13.3 %collective-permute-start.8 = (bf16[16,7296]{1,0:T(8,128)(2,1)}, bf16[16,7296]{1,0:T(8,128)(2,1)S(1)}, u32[]{:S(2)}, u32[]{:S(2)}) collective-permute-start(bf16[16,7296]{1,0:T(8,128)(2,1)} %pack.1.refs_12_), channel_id=1, source_target_pairs={{0,4},{1,5},{2,6},{3,7},{4,0},{5,1},{6,2},{7,3},{8,12},{9,13},{10,... | collective-permute-start | bytes 700424 | tf_op jit(solution)/shard_map/ppermute | solution.py:23
  6.3 19.7 %collective-permute-start.4 = (bf16[16,7296]{1,0:T(8,128)(2,1)}, bf16[16,7296]{1,0:T(8,128)(2,1)S(1)}, u32[]{:S(2)}, u32[]{:S(2)}) collective-permute-start(bf16[16,7296]{1,0:T(8,128)(2,1)} %pack.1.refs_12_), channel_id=1, source_target_pairs={{0,8},{1,9},{2,10},{3,11},{4,12},{5,13},{6,14},{7,15},{8,0},{9,1},... | collective-permute-start | bytes 700424 | tf_op jit(solution)/shard_map/ppermute | solution.py:23
  8.9 17.7 %collective-permute-start = (bf16[16,7296]{1,0:T(8,128)(2,1)}, bf16[16,7296]{1,0:T(8,128)(2,1)S(1)}, u32[]{:S(2)}, u32[]{:S(2)}) collective-permute-start(bf16[16,7296]{1,0:T(8,128)(2,1)} %pack.1.refs_12_), channel_id=1, source_target_pairs={{0,12},{1,13},{2,14},{3,15},{4,8},{5,9},{6,10},{7,11},{8,4},{9,5},... | collective-permute-start | bytes 700424 | tf_op jit(solution)/shard_map/ppermute | solution.py:23
  10.7 25.9 %copy-start.2 = (bf16[16,7296]{1,0:T(8,128)(2,1)}, bf16[16,7296]{1,0:T(8,128)(2,1)S(1)}, u32[]{:S(2)}) copy-start(bf16[16,7296]{1,0:T(8,128)(2,1)S(1)} %collective-permute-done.9.refs_13_) | copy-start | bytes 700420
  10.7 17.5 %collective-permute-start.14 = (bf16[16,7296]{1,0:T(8,128)(2,1)S(1)}, bf16[16,7296]{1,0:T(8,128)(2,1)S(1)}, u32[]{:S(2)}, u32[]{:S(2)}) collective-permute-start(bf16[16,7296]{1,0:T(8,128)(2,1)S(1)} %collective-permute-done.9.refs_13_), channel_id=1, source_target_pairs={{0,1},{1,0},{2,3},{3,2},{4,5},{5,4},{6,7},{7,6},{8,9},{9,8},{10,11... | collective-permute-start | bytes 700424 | tf_op jit(solution)/shard_map/ppermute | solution.py:23
  10.7 25.9 %copy-start.3 = (bf16[16,7296]{1,0:T(8,128)(2,1)}, bf16[16,7296]{1,0:T(8,128)(2,1)S(1)}, u32[]{:S(2)}) copy-start(bf16[16,7296]{1,0:T(8,128)(2,1)S(1)} %collective-permute-done.13.refs_14_) | copy-start | bytes 700420
  10.7 17.4 %collective-permute-start.10 = (bf16[16,7296]{1,0:T(8,128)(2,1)S(1)}, bf16[16,7296]{1,0:T(8,128)(2,1)S(1)}, u32[]{:S(2)}, u32[]{:S(2)}) collective-permute-start(bf16[16,7296]{1,0:T(8,128)(2,1)S(1)} %collective-permute-done.9.refs_13_), channel_id=1, source_target_pairs={{0,4},{1,5},{2,6},{3,7},{4,0},{5,1},{6,2},{7,3},{8,12},{9,13},{10,... | collective-permute-start | bytes 700424 | tf_op jit(solution)/shard_map/ppermute | solution.py:23
  18.1 18.5 %copy-start.4 = (bf16[16,7296]{1,0:T(8,128)(2,1)}, bf16[16,7296]{1,0:T(8,128)(2,1)S(1)}, u32[]{:S(2)}) copy-start(bf16[16,7296]{1,0:T(8,128)(2,1)S(1)} %collective-permute-done.8.refs_8_) | copy-start | bytes 700420
  18.1 10.6 %collective-permute-start.11 = (bf16[16,7296]{1,0:T(8,128)(2,1)S(1)}, bf16[16,7296]{1,0:T(8,128)(2,1)S(1)}, u32[]{:S(2)}, u32[]{:S(2)}) collective-permute-start(bf16[16,7296]{1,0:T(8,128)(2,1)S(1)} %collective-permute-done.8.refs_8_), channel_id=1, source_target_pairs={{0,1},{1,0},{2,3},{3,2},{4,5},{5,4},{6,7},{7,6},{8,9},{9,8},{10,11... | collective-permute-start | bytes 700424 | tf_op jit(solution)/shard_map/ppermute | solution.py:23
  26.1 10.5 %copy-start.5 = (bf16[16,7296]{1,0:T(8,128)(2,1)}, bf16[16,7296]{1,0:T(8,128)(2,1)S(1)}, u32[]{:S(2)}) copy-start(bf16[16,7296]{1,0:T(8,128)(2,1)S(1)} %collective-permute-done.4.refs_4_) | copy-start | bytes 700420
  26.1 6.4 %collective-permute-start.5 = (bf16[16,7296]{1,0:T(8,128)(2,1)S(1)}, bf16[16,7296]{1,0:T(8,128)(2,1)S(1)}, u32[]{:S(2)}, u32[]{:S(2)}) collective-permute-start(bf16[16,7296]{1,0:T(8,128)(2,1)S(1)} %collective-permute-done.4.refs_4_), channel_id=1, source_target_pairs={{0,2},{1,3},{2,0},{3,1},{4,6},{5,7},{6,4},{7,5},{8,10},{9,11},{10,... | collective-permute-start | bytes 700424 | tf_op jit(solution)/shard_map/ppermute | solution.py:23
  26.6 10.0 %copy-start.6 = (bf16[16,7296]{1,0:T(8,128)(2,1)}, bf16[16,7296]{1,0:T(8,128)(2,1)S(1)}, u32[]{:S(2)}) copy-start(bf16[16,7296]{1,0:T(8,128)(2,1)S(1)} %collective-permute-done.refs_0_) | copy-start | bytes 700420
  26.6 8.4 %collective-permute-start.1 = (bf16[16,7296]{1,0:T(8,128)(2,1)S(1)}, bf16[16,7296]{1,0:T(8,128)(2,1)S(1)}, u32[]{:S(2)}, u32[]{:S(2)}) collective-permute-start(bf16[16,7296]{1,0:T(8,128)(2,1)S(1)} %collective-permute-done.refs_0_), channel_id=1, source_target_pairs={{0,2},{1,3},{2,0},{3,1},{4,6},{5,7},{6,4},{7,5},{8,10},{9,11},{10,... | collective-permute-start | bytes 700424 | tf_op jit(solution)/shard_map/ppermute | solution.py:23
  28.1 8.4 %copy-start.7 = (bf16[16,7296]{1,0:T(8,128)(2,1)}, bf16[16,7296]{1,0:T(8,128)(2,1)S(1)}, u32[]{:S(2)}) copy-start(bf16[16,7296]{1,0:T(8,128)(2,1)S(1)} %collective-permute-done.14.refs_15_) | copy-start | bytes 700420
  28.1 6.9 %collective-permute-start.6 = (bf16[16,7296]{1,0:T(8,128)(2,1)S(1)}, bf16[16,7296]{1,0:T(8,128)(2,1)S(1)}, u32[]{:S(2)}, u32[]{:S(2)}) collective-permute-start(bf16[16,7296]{1,0:T(8,128)(2,1)S(1)} %collective-permute-done.4.refs_4_), channel_id=1, source_target_pairs={{0,1},{1,0},{2,3},{3,2},{4,5},{5,4},{6,7},{7,6},{8,9},{9,8},{10,11... | collective-permute-start | bytes 700424 | tf_op jit(solution)/shard_map/ppermute | solution.py:23
  28.1 6.9 %collective-permute-start.2 = (bf16[16,7296]{1,0:T(8,128)(2,1)S(1)}, bf16[16,7296]{1,0:T(8,128)(2,1)S(1)}, u32[]{:S(2)}, u32[]{:S(2)}) collective-permute-start(bf16[16,7296]{1,0:T(8,128)(2,1)S(1)} %collective-permute-done.refs_0_), channel_id=1, source_target_pairs={{0,1},{1,0},{2,3},{3,2},{4,5},{5,4},{6,7},{7,6},{8,9},{9,8},{10,11... | collective-permute-start | bytes 700424 | tf_op jit(solution)/shard_map/ppermute | solution.py:23
  28.6 6.4 %collective-permute-start.12 = (bf16[16,7296]{1,0:T(8,128)(2,1)S(1)}, bf16[16,7296]{1,0:T(8,128)(2,1)S(1)}, u32[]{:S(2)}, u32[]{:S(2)}) collective-permute-start(bf16[16,7296]{1,0:T(8,128)(2,1)S(1)} %collective-permute-done.10.refs_9_), channel_id=1, source_target_pairs={{0,1},{1,0},{2,3},{3,2},{4,5},{5,4},{6,7},{7,6},{8,9},{9,8},{10,11... | collective-permute-start | bytes 700424 | tf_op jit(solution)/shard_map/ppermute | solution.py:23
  32.5 2.6 %collective-permute-start.7 = (bf16[16,7296]{1,0:T(8,128)(2,1)S(1)}, bf16[16,7296]{1,0:T(8,128)(2,1)S(1)}, u32[]{:S(2)}, u32[]{:S(2)}) collective-permute-start(bf16[16,7296]{1,0:T(8,128)(2,1)S(1)} %collective-permute-done.5.refs_5_), channel_id=1, source_target_pairs={{0,1},{1,0},{2,3},{3,2},{4,5},{5,4},{6,7},{7,6},{8,9},{9,8},{10,11... | collective-permute-start | bytes 700424 | tf_op jit(solution)/shard_map/ppermute | solution.py:23
  35.0 1.5 %collective-permute-start.3 = (bf16[16,7296]{1,0:T(8,128)(2,1)S(1)}, bf16[16,7296]{1,0:T(8,128)(2,1)S(1)}, u32[]{:S(2)}, u32[]{:S(2)}) collective-permute-start(bf16[16,7296]{1,0:T(8,128)(2,1)S(1)} %collective-permute-done.1.refs_1_), channel_id=1, source_target_pairs={{0,1},{1,0},{2,3},{3,2},{4,5},{5,4},{6,7},{7,6},{8,9},{9,8},{10,11... | collective-permute-start | bytes 700424 | tf_op jit(solution)/shard_map/ppermute | solution.py:23
  55.1 2.1 %collective-permute-start.15 = (bf16[32,7168]{1,0:T(8,128)(2,1)}, bf16[32,7168]{1,0:T(8,128)(2,1)S(1)}, u32[]{:S(2)}, u32[]{:S(2)}) collective-permute-start(bf16[32,7168]{1,0:T(8,128)(2,1)} %get-tuple-element.16), channel_id=1, source_target_pairs={{0,1},{1,0},{2,3},{3,2},{4,5},{5,4},{6,7},{7,6},{8,9},{9,8},{10,11... | collective-permute-start | bytes 1376264 | tf_op jit(solution)/shard_map/ppermute | solution.py:23
  58.9 9.9 %collective-permute-start.16 = (bf16[16,7168]{1,0:T(8,128)(2,1)S(1)}, bf16[16,7168]{1,0:T(8,128)(2,1)S(1)}, u32[]{:S(2)}, u32[]{:S(2)}) collective-permute-start(bf16[16,7168]{1,0:T(8,128)(2,1)S(1)} %slice.57), channel_id=1, source_target_pairs={{0,2},{1,3},{2,0},{3,1},{4,6},{5,7},{6,4},{7,5},{8,10},{9,11},{10,... | collective-permute-start | bytes 688136 | tf_op jit(solution)/shard_map/ppermute | solution.py:23
  67.5 7.5 %collective-permute-start.18 = (bf16[32,7168]{1,0:T(8,128)(2,1)S(1)}, bf16[32,7168]{1,0:T(8,128)(2,1)S(1)}, u32[]{:S(2)}, u32[]{:S(2)}) collective-permute-start(bf16[32,7168]{1,0:T(8,128)(2,1)S(1)} %get-tuple-element.20), channel_id=1, source_target_pairs={{0,1},{1,0},{2,3},{3,2},{4,5},{5,4},{6,7},{7,6},{8,9},{9,8},{10,11... | collective-permute-start | bytes 1376264 | tf_op jit(solution)/shard_map/ppermute | solution.py:23
  67.6 8.7 %collective-permute-start.21 = (bf16[32,7168]{1,0:T(8,128)(2,1)S(1)}, bf16[32,7168]{1,0:T(8,128)(2,1)S(1)}, u32[]{:S(2)}, u32[]{:S(2)}) collective-permute-start(bf16[32,7168]{1,0:T(8,128)(2,1)S(1)} %get-tuple-element.22), channel_id=1, source_target_pairs={{0,1},{1,0},{2,3},{3,2},{4,5},{5,4},{6,7},{7,6},{8,9},{9,8},{10,11... | collective-permute-start | bytes 1376264 | tf_op jit(solution)/shard_map/ppermute | solution.py:23
  68.1 11.7 %collective-permute-start.24 = (bf16[32,7168]{1,0:T(8,128)(2,1)S(1)}, bf16[32,7168]{1,0:T(8,128)(2,1)S(1)}, u32[]{:S(2)}, u32[]{:S(2)}) collective-permute-start(bf16[32,7168]{1,0:T(8,128)(2,1)S(1)} %get-tuple-element.24), channel_id=1, source_target_pairs={{0,1},{1,0},{2,3},{3,2},{4,5},{5,4},{6,7},{7,6},{8,9},{9,8},{10,11... | collective-permute-start | bytes 1376264 | tf_op jit(solution)/shard_map/ppermute | solution.py:23
  69.4 22.3 %collective-permute-start.17 = (bf16[16,7168]{1,0:T(8,128)(2,1)S(1)}, bf16[16,7168]{1,0:T(8,128)(2,1)S(1)}, u32[]{:S(2)}, u32[]{:S(2)}) collective-permute-start(bf16[16,7168]{1,0:T(8,128)(2,1)S(1)} %add_convert_fusion.8), channel_id=1, source_target_pairs={{0,12},{1,13},{2,14},{3,15},{4,8},{5,9},{6,10},{7,11},{8,4},{9,5},... | collective-permute-start | bytes 688136 | tf_op jit(solution)/shard_map/ppermute | solution.py:23
  77.0 8.5 %collective-permute-start.19 = (bf16[16,7168]{1,0:T(8,128)(2,1)S(1)}, bf16[16,7168]{1,0:T(8,128)(2,1)S(1)}, u32[]{:S(2)}, u32[]{:S(2)}) collective-permute-start(bf16[16,7168]{1,0:T(8,128)(2,1)S(1)} %slice.60), channel_id=1, source_target_pairs={{0,2},{1,3},{2,0},{3,1},{4,6},{5,7},{6,4},{7,5},{8,10},{9,11},{10,... | collective-permute-start | bytes 688136 | tf_op jit(solution)/shard_map/ppermute | solution.py:23
  79.2 11.2 %collective-permute-start.22 = (bf16[16,7168]{1,0:T(8,128)(2,1)S(1)}, bf16[16,7168]{1,0:T(8,128)(2,1)S(1)}, u32[]{:S(2)}, u32[]{:S(2)}) collective-permute-start(bf16[16,7168]{1,0:T(8,128)(2,1)S(1)} %slice.64), channel_id=1, source_target_pairs={{0,2},{1,3},{2,0},{3,1},{4,6},{5,7},{6,4},{7,5},{8,10},{9,11},{10,... | collective-permute-start | bytes 688136 | tf_op jit(solution)/shard_map/ppermute | solution.py:23
  80.0 14.6 %collective-permute-start.25 = (bf16[16,7168]{1,0:T(8,128)(2,1)S(1)}, bf16[16,7168]{1,0:T(8,128)(2,1)S(1)}, u32[]{:S(2)}, u32[]{:S(2)}) collective-permute-start(bf16[16,7168]{1,0:T(8,128)(2,1)S(1)} %slice.68), channel_id=1, source_target_pairs={{0,2},{1,3},{2,0},{3,1},{4,6},{5,7},{6,4},{7,5},{8,10},{9,11},{10,... | collective-permute-start | bytes 688136 | tf_op jit(solution)/shard_map/ppermute | solution.py:23
  86.1 11.1 %collective-permute-start.20 = (bf16[16,7168]{1,0:T(8,128)(2,1)S(1)}, bf16[16,7168]{1,0:T(8,128)(2,1)S(1)}, u32[]{:S(2)}, u32[]{:S(2)}) collective-permute-start(bf16[16,7168]{1,0:T(8,128)(2,1)S(1)} %add_convert_fusion.7), channel_id=1, source_target_pairs={{0,8},{1,9},{2,10},{3,11},{4,12},{5,13},{6,14},{7,15},{8,0},{9,1},... | collective-permute-start | bytes 688136 | tf_op jit(solution)/shard_map/ppermute | solution.py:23
  90.5 10.5 %collective-permute-start.23 = (bf16[16,7168]{1,0:T(8,128)(2,1)S(1)}, bf16[16,7168]{1,0:T(8,128)(2,1)S(1)}, u32[]{:S(2)}, u32[]{:S(2)}) collective-permute-start(bf16[16,7168]{1,0:T(8,128)(2,1)S(1)} %add_convert_fusion.6), channel_id=1, source_target_pairs={{0,4},{1,5},{2,6},{3,7},{4,0},{5,1},{6,2},{7,3},{8,12},{9,13},{10,... | collective-permute-start | bytes 688136 | tf_op jit(solution)/shard_map/ppermute | solution.py:23
  (11 other events, 30.7 us)

commit v2 on v0

v2 whole, which is shorter than its diff:
```python
import functools

import jax
import jax.numpy as jnp
from jax import lax
from jax.experimental import pallas as pl
from jax.experimental.pallas import tpu as pltpu
from jax.sharding import PartitionSpec as P

E = 16
CAP = 8
LANES = 128
RING = 7
EARLY = 6
denominator = 64.0
VMEM = pl.BlockSpec(memory_space=pltpu.VMEM)
SMEM = pl.BlockSpec(memory_space=pltpu.SMEM)
ANY = pl.BlockSpec(memory_space=pl.ANY)
HBM = pl.BlockSpec(memory_space=pltpu.HBM)


def exchange(x, distance):
    n = lax.axis_size("local")
    return lax.ppermute(x, "local", [(i, i ^ distance) for i in range(n)])


def pack_kernel(rows_ref, routes_ref, comb_ref, out_ref):
    rows, width = rows_ref.shape
    out_ref[:, :width] = rows_ref[...]
    sub = lax.broadcasted_iota(jnp.int32, (LANES, rows), 0)
    table = jnp.zeros((LANES, rows), jnp.int32)
    for k in range(routes_ref.shape[0]):
        table = jnp.where(sub == routes_ref[k : k + 1, :], comb_ref[k : k + 1, :], table)
    same = lax.broadcasted_iota(jnp.int32, (rows, rows), 0) == lax.broadcasted_iota(jnp.int32, (rows, rows), 1)
    turned = lax.dot_general(
        same.astype(jnp.float32).astype(jnp.bfloat16),
        table.astype(jnp.float32).astype(jnp.bfloat16),
        (((1,), (1,)), ((), ())), preferred_element_type=jnp.float32,
    )
    out_ref[:, width:] = turned.astype(jnp.bfloat16)


def pack(rows, routes, comb):
    return pl.pallas_call(
        pack_kernel,
        out_shape=jax.ShapeDtypeStruct((rows.shape[0], rows.shape[1] + LANES), rows.dtype),
        in_specs=[VMEM] * 3,
        out_specs=VMEM,
        name="pack",
    )(rows, routes.T, comb.T)


def routing(table, expert, block):
    count = table.shape[0]
    slots = count // block * CAP
    mine = (lax.broadcasted_iota(jnp.int32, (8, LANES), 1) == expert).astype(jnp.float32)
    along = lax.dot_general(
        mine.astype(jnp.bfloat16), table, (((1,), (1,)), ((), ())),
        preferred_element_type=jnp.float32,
    )
    down = jnp.sum(table.astype(jnp.float32) * mine[:1, :], axis=1, keepdims=True)
    r = lax.broadcasted_iota(jnp.int32, (count, count), 0)
    s = lax.broadcasted_iota(jnp.int32, (count, count), 1)
    same = (r // block) == (s // block)
    before = (same & (r < s)).astype(jnp.float32).astype(jnp.bfloat16)
    after = (same & (s < r)).astype(jnp.float32).astype(jnp.bfloat16)
    chosen = (along > 0).astype(jnp.float32)
    rank = jnp.dot(chosen.astype(jnp.bfloat16), before, preferred_element_type=jnp.float32)
    start = (lax.broadcasted_iota(jnp.int32, (8, count), 1) // block) * CAP
    slot = jnp.where(along > 0, rank.astype(jnp.int32) + start, slots)[:1, :]
    place = (lax.broadcasted_iota(jnp.int32, (slots, count), 0) == slot)
    place = place.astype(jnp.float32).astype(jnp.bfloat16)
    chosen = jnp.broadcast_to((down > 0).astype(jnp.float32), (count, LANES))
    rank = jnp.dot(after, chosen.astype(jnp.bfloat16), preferred_element_type=jnp.float32)
    start = (lax.broadcasted_iota(jnp.int32, (count, 1), 0) // block) * CAP
    slot = rank[:, :1].astype(jnp.int32) + start
    combine = jnp.where(
        lax.broadcasted_iota(jnp.int32, (count, slots), 1) == slot, down / denominator, 0.0
    ).astype(jnp.bfloat16)
    return place, combine


def block_copies(block_refs, rows_ref, sems):
    block = block_refs[0].shape[0]
    return [
        pltpu.make_async_copy(ref, rows_ref.at[pl.ds(i * block, block), :], sems.at[i])
        for i, ref in enumerate(block_refs)
    ]


def weight_pieces(gate_hbm, up_hbm, down_hbm, deep, steps):
    cuts = [pl.ds(j * deep, deep) for j in range(steps)]
    pieces = [hbm.at[c, :] for c in cuts for hbm in (gate_hbm, up_hbm)]
    return cuts, pieces + [down_hbm.at[:, c] for c in cuts]


def early_kernel(blocks, expert_ref, *refs):
    block_refs, refs = refs[:blocks], refs[blocks:]
    gate_hbm, up_hbm, items_ref, combine_ref, first_ref = refs[:5]
    rows_ref, sems, weight_sems = refs[5:]
    ahead, deep = first_ref.shape[:2]
    width = items_ref.shape[1]
    steps = width // deep
    copies = block_copies(block_refs, rows_ref, sems)
    pieces = [hbm.at[pl.ds(j * deep, deep), :] for j in range(steps) for hbm in (gate_hbm, up_hbm)]
    near = [
        pltpu.make_async_copy(pieces[i], first_ref.at[i], weight_sems.at[i]) for i in range(ahead)
    ]
    for copy in copies + near:
        copy.start()
    for copy in copies:
        copy.wait()
    place, combine = routing(rows_ref[:, width:], expert_ref[0], block_refs[0].shape[0])
    combine_ref[...] = combine
    for j in range(steps):
        c = pl.ds(j * deep, deep)
        items = jnp.dot(place, rows_ref[:, c], preferred_element_type=jnp.float32)
        items_ref[:, c] = items.astype(jnp.bfloat16)
    for copy in near:
        copy.wait()


def early_part(expert, blocks, w_gate, w_up):
    n = len(blocks)
    block, total = blocks[0].shape
    width, units = total - LANES, w_gate.shape[1]
    slots = n * CAP
    limit = 2 * n * block * total + 4 * slots * width + (6 << 20)
    items, combine, first = pl.pallas_call(
        functools.partial(early_kernel, n),
        out_shape=[
            jax.ShapeDtypeStruct((slots, width), jnp.bfloat16),
            jax.ShapeDtypeStruct((n * block, slots), jnp.bfloat16),
            pltpu.VMEM((EARLY, units, units), jnp.bfloat16),
        ],
        in_specs=[SMEM] + [ANY] * n + [HBM, HBM],
        out_specs=[VMEM] * 3,
        scratch_shapes=[
            pltpu.VMEM((n * block, total), jnp.bfloat16),
            pltpu.SemaphoreType.DMA((n,)),
            pltpu.SemaphoreType.DMA((EARLY,)),
        ],
        compiler_params=pltpu.CompilerParams(vmem_limit_bytes=limit),
        cost_estimate=pl.CostEstimate(
            flops=2 * slots * n * block * width,
            bytes_accessed=EARLY * units * units * 2,
            transcendentals=0,
        ),
        name="early",
    )(expert, *blocks, w_gate, w_up)
    return items, combine, pltpu.with_memory_space_constraint(first, pltpu.VMEM)


def expert_kernel(blocks, expert_ref, *refs):
    block_refs, refs = refs[:blocks], refs[blocks:]
    items_ref, combine_ref, first_ref, gate_hbm, up_hbm, down_hbm = refs[:6]
    outs, refs = refs[6:-7], refs[-7:]
    rows_ref, hidden_ref, ring_ref, gate_sum, up_sum, sems, weight_sems = refs
    ahead = first_ref.shape[0]
    block, width = outs[0].shape
    slots, deep = hidden_ref.shape
    steps = width // deep
    ready = items_ref.shape[0]
    copies = block_copies(block_refs, rows_ref, sems)
    cuts, pieces = weight_pieces(gate_hbm, up_hbm, down_hbm, deep, steps)
    near = [
        pltpu.make_async_copy(piece, ring_ref.at[i % RING], weight_sems.at[i % RING])
        for i, piece in enumerate(pieces[ahead:])
    ]
    for copy in copies + near[: RING - 1]:
        copy.start()
    for copy in copies:
        copy.wait()
    place, combine = routing(rows_ref[:, width:], expert_ref[0], block)

    def weights(i):
        if i < ahead:
            return first_ref[i]
        i -= ahead
        near[i].wait()
        if i + RING - 1 < len(near):
            near[i + RING - 1].start()
        return ring_ref[i % RING]

    for j, c in enumerate(cuts):
        items = jnp.dot(place, rows_ref[:, c], preferred_element_type=jnp.float32)
        items = jnp.concatenate([items_ref[:, c], items.astype(jnp.bfloat16)], axis=0)
        gate = jnp.dot(items, weights(2 * j), preferred_element_type=jnp.float32)
        up = jnp.dot(items, weights(2 * j + 1), preferred_element_type=jnp.float32)
        if j > 0:
            gate, up = gate_sum[...] + gate, up_sum[...] + up
        gate_sum[...], up_sum[...] = gate, up
    gate = gate_sum[...]
    hidden_ref[...] = (gate / (1.0 + jnp.exp(-gate)) * up_sum[...]).astype(jnp.bfloat16)

    for j, c in enumerate(cuts):
        piece = jnp.dot(hidden_ref[...], weights(2 * steps + j), preferred_element_type=jnp.float32)
        piece = piece.astype(jnp.bfloat16)
        part = jnp.dot(combine_ref[...], piece[:ready], preferred_element_type=jnp.float32)
        rest = jnp.dot(combine, piece[ready:], preferred_element_type=jnp.float32)
        part, rest = part.astype(jnp.bfloat16), rest.astype(jnp.bfloat16)
        for i, out in enumerate(outs):
            k = i * block
            out[:, c] = part[k : k + block] if k < part.shape[0] else rest[k - part.shape[0] :][:block]


def expert_part(expert, blocks, early, w_gate, w_up, w_down):
    n = len(blocks)
    block, total = blocks[0].shape
    width, units = total - LANES, w_gate.shape[1]
    slots = early[0].shape[0] + n * CAP
    outs = early[1].shape[0] // block + n
    flops = 2 * slots * units * width * 3
    weights = [pltpu.with_memory_space_constraint(w, pltpu.HBM) for w in (w_gate, w_up, w_down)]
    limit = 2 * RING * units * units + 8 * slots * units + 2 * outs * block * width + (8 << 20)
    return pl.pallas_call(
        functools.partial(expert_kernel, n),
        out_shape=[jax.ShapeDtypeStruct((block, width), jnp.bfloat16)] * outs,
        in_specs=[SMEM] + [ANY] * n + [VMEM] * 3 + [HBM] * 3,
        out_specs=[VMEM] * outs,
        scratch_shapes=[
            pltpu.VMEM((n * block, total), jnp.bfloat16),
            pltpu.VMEM((slots, units), jnp.bfloat16),
            pltpu.VMEM((RING, units, units), jnp.bfloat16),
            pltpu.VMEM((slots, units), jnp.float32),
            pltpu.VMEM((slots, units), jnp.float32),
            pltpu.SemaphoreType.DMA((n,)),
            pltpu.SemaphoreType.DMA((RING,)),
        ],
        compiler_params=pltpu.CompilerParams(vmem_limit_bytes=limit),
        cost_estimate=pl.CostEstimate(
            flops=flops, bytes_accessed=w_down.size * 6, transcendentals=0
        ),
        name="expert",
    )(expert, *blocks, *early, *weights)


def add_kernel(count, *refs):
    total = refs[0][...].astype(jnp.float32)
    for term in refs[1:count]:
        total = total + term[...].astype(jnp.float32)
    refs[-1][...] = total.astype(refs[-1].dtype)


def add(terms, after=()):
    return pl.pallas_call(
        functools.partial(add_kernel, len(terms)),
        out_shape=jax.ShapeDtypeStruct(terms[0].shape, jnp.bfloat16),
        in_specs=[VMEM] * len(terms) + [ANY] * len(after),
        out_specs=VMEM,
        compiler_params=pltpu.CompilerParams(vmem_limit_bytes=4 << 20),
        cost_estimate=pl.CostEstimate(flops=1, bytes_accessed=1, transcendentals=0),
        name="add",
    )(*terms, *after)


def on_device(rows_in, routes, comb_num, w_gate, w_up, w_down):
    n = lax.axis_size("local")
    me = lax.axis_index("local")
    expert = (me // (n // E)).astype(jnp.int32).reshape(1)
    planes = range(n - 4, -1, -4)

    own = pack(rows_in, routes, comb_num)
    got = {0: own}
    for k in planes[:-1]:
        got[k] = exchange(own, k)
    got[2] = exchange(own, 2)
    got[1] = exchange(own, 1)
    first, second = planes[0], planes[1]
    soon = [k | i for k in (first, 0) for i in range(4)]
    late = [k | i for k in planes[1:-1] for i in range(4)]
    got[first | 2] = exchange(got[first], 2)
    for k in soon:
        if k % 2:
            got[k] = exchange(got[k - 1], 1)
    weights = [pltpu.with_memory_space_constraint(w, pltpu.HBM) for w in (w_gate, w_up)]
    items, *early = early_part(expert, [got[k] for k in soon], *weights)
    source, items = lax.optimization_barrier((got[second], items))
    for k in planes[1:-1]:
        got[k | 2] = exchange(source if k == second else got[k], 2)
    for k in late:
        if k % 2:
            got[k] = exchange(got[k - 1], 1)
    outs = expert_part(expert, [got[k] for k in late], (items, *early), w_gate, w_up, w_down)
    parts = dict(zip(soon + late, outs))

    def pair(k, after=()):
        return exchange(add([parts[k | 2], exchange(parts[k | 3], 1)], after), 2)

    def home(k, come, after):
        return add([parts[k], exchange(parts[k | 1], 1), come], after)

    turns = [first, 4, *planes[1:-2]]
    come = {k: pair(k) for k in turns}
    halves = {k: home(k, come[k], ()) for k in turns}
    came = {k: exchange(halves[k], k) for k in turns}
    come[0] = pair(0, (came[first], *halves.values()))
    return add([home(0, come[0], ()), *came.values()])


def solution(mesh):
    in_specs = (
        P(("parts", "local"), None),
        P(("parts", "local"), None),
        P(("parts", "local"), None),
        P(None, "local"),
        P(None, "local"),
        P("local", None),
    )
    out_specs = P(("parts", "local"), None)
    return jax.shard_map(
        on_device, mesh=mesh, in_specs=in_specs, out_specs=out_specs, check_vma=False
    )
```

time: 116 us -> 93.1 us (0.80)
  the two profiles are of different devices: /device:TPU:15 before, /device:TPU:0 now
where the time goes in v2:
time: 93.1 us; the launch traced here: 92.9 us
  waiting for transfers between devices  39.7 us (43%)
  starting transfers between devices  27.9 us (30%)
  Pallas kernels  24.2 us (26%)
    ppermute x30, waiting for transfers between devices, exchange(): return lax.ppermute(x, 'local', [(i, i ^ distance) for i in range(n)])  39.7 us
    ppermute x30, starting transfers between devices, exchange(): return lax.ppermute(x, 'local', [(i, i ^ distance) for i in range(n)])  27.9 us
    pallas_call x1, Pallas kernels, expert_part(): pl.pallas_call(functools.partial(expert_kernel, n), out_shape=[jax.ShapeD...  13.9 us
    pallas_call x1, Pallas kernels, early_part(): pl.pallas_call(functools.partial(early_kernel, n), out_shape=[jax.ShapeDt...  7.15 us
  transfers between devices with their start and end apart: 30, of which 14 were waited for; matrix products, arithmetic and copies ran while one was open for 0% of the time, Pallas kernels for 8%

profile of v2, /device:TPU:0, one launch (start us, length us, event | category | flops | bytes accessed | tf_op | source)
XLA Modules:
  0.0 92.9 jit_solution(17054298085670456364)
XLA Ops:
  0.0 1.8 %pack.1.refs_4_ = bf16[16,7296]{1,0:T(8,128)(2,1)} custom-call(bf16[16,7168]{1,0:T(8,128)(2,1)} %rows_ref.1, s32[4,16]{1,0:T(4,128)} %bitcast.3, s32[4,16]{1,0:T(4,128)} %bitcast.4), custom_call_target="tpu_custom_call" | custom-call | tf_op jit(solution)/shard_map/pack/pallas_call | solution.py:44
  1.8 5.0 %collective-permute-start.2 = (bf16[16,7296]{1,0:T(8,128)(2,1)}, bf16[16,7296]{1,0:T(8,128)(2,1)S(1)}, u32[]{:S(2)}, u32[]{:S(2)}) collective-permute-start(bf16[16,7296]{1,0:T(8,128)(2,1)} %pack.1.refs_4_), channel_id=1, source_target_pairs={{0,12},{1,13},{2,14},{3,15},{4,8},{5,9},{6,10},{7,11},{8,4},{9,5},... | collective-permute-start | bytes 700424 | tf_op jit(solution)/shard_map/ppermute | solution.py:24
  6.9 1.5 %collective-permute-start.7 = (bf16[16,7296]{1,0:T(8,128)(2,1)}, bf16[16,7296]{1,0:T(8,128)(2,1)S(1)}, u32[]{:S(2)}, u32[]{:S(2)}) collective-permute-start(bf16[16,7296]{1,0:T(8,128)(2,1)} %pack.1.refs_4_), channel_id=1, source_target_pairs={{0,2},{1,3},{2,0},{3,1},{4,6},{5,7},{6,4},{7,5},{8,10},{9,11},{10,... | collective-permute-start | bytes 700424 | tf_op jit(solution)/shard_map/ppermute | solution.py:24
  8.4 4.5 %collective-permute-done.2.refs_0_ = bf16[16,7296]{1,0:T(8,128)(2,1)S(1)} collective-permute-done((bf16[16,7296]{1,0:T(8,128)(2,1)}, bf16[16,7296]{1,0:T(8,128)(2,1)S(1)}, u32[]{:S(2)}, u32[]{:S(2)}) %collective-permute-start.2) | collective-permute-done | bytes 233504 | tf_op jit(solution)/shard_map/ppermute | solution.py:24
  12.9 1.5 %collective-permute-start.4 = (bf16[16,7296]{1,0:T(8,128)(2,1)S(1)}, bf16[16,7296]{1,0:T(8,128)(2,1)S(1)}, u32[]{:S(2)}, u32[]{:S(2)}) collective-permute-start(bf16[16,7296]{1,0:T(8,128)(2,1)S(1)} %collective-permute-done.2.refs_0_), channel_id=1, source_target_pairs={{0,2},{1,3},{2,0},{3,1},{4,6},{5,7},{6,4},{7,5},{8,10},{9,11},{10,... | collective-permute-start | bytes 700424 | tf_op jit(solution)/shard_map/ppermute | solution.py:24
  14.4 4.6 %collective-permute-start.11 = (bf16[16,7296]{1,0:T(8,128)(2,1)}, bf16[16,7296]{1,0:T(8,128)(2,1)S(1)}, u32[]{:S(2)}, u32[]{:S(2)}) collective-permute-start(bf16[16,7296]{1,0:T(8,128)(2,1)} %pack.1.refs_4_), channel_id=1, source_target_pairs={{0,4},{1,5},{2,6},{3,7},{4,0},{5,1},{6,2},{7,3},{8,12},{9,13},{10,... | collective-permute-start | bytes 700424 | tf_op jit(solution)/shard_map/ppermute | solution.py:24
  19.0 0.5 collective-permute-start.3
  20.0 3.9 %collective-permute-done.11.refs_4_ = bf16[16,7296]{1,0:T(8,128)(2,1)S(1)} collective-permute-done((bf16[16,7296]{1,0:T(8,128)(2,1)}, bf16[16,7296]{1,0:T(8,128)(2,1)S(1)}, u32[]{:S(2)}, u32[]{:S(2)}) %collective-permute-start.11) | collective-permute-done | bytes 233504 | tf_op jit(solution)/shard_map/ppermute | solution.py:24
  23.9 2.6 %collective-permute-start = (bf16[16,7296]{1,0:T(8,128)(2,1)}, bf16[16,7296]{1,0:T(8,128)(2,1)S(1)}, u32[]{:S(2)}, u32[]{:S(2)}) collective-permute-start(bf16[16,7296]{1,0:T(8,128)(2,1)} %pack.1.refs_4_), channel_id=1, source_target_pairs={{0,8},{1,9},{2,10},{3,11},{4,12},{5,13},{6,14},{7,15},{8,0},{9,1},... | collective-permute-start | bytes 700424 | tf_op jit(solution)/shard_map/ppermute | solution.py:24
  27.0 0.9 %copy-done = bf16[16,7296]{1,0:T(8,128)(2,1)S(1)} copy-done((bf16[16,7296]{1,0:T(8,128)(2,1)S(1)}, bf16[16,7296]{1,0:T(8,128)(2,1)}, u32[]{:S(2)}) %copy-start) | copy-done | bytes 233496
  28.0 7.1 %early.1 = (bf16[64,7168]{1,0:T(8,128)(2,1)S(1)}, bf16[128,64]{1,0:T(8,128)(2,1)S(1)}, bf16[6,1024,1024]{2,1,0:T(8,128)(2,1)S(1)}) custom-call(s32[1]{0:T(128)} %bitcast.expert_ref, bf16[16,7296]{1,0:T(8,128)(2,1)S(1)} %collective-permute-done.2.refs_0_, bf16[16,7296]{1,0:T(8,128)(2,1)S(1)} %collective-permute-done.3.refs_1_, ...), custom_call_target="tpu_custom_call" | custom-call | flops 117440512 | bytes 12582912 | tf_op jit(solution)/shard_map/early/pallas_call | solution.py:129
  35.1 1.5 %collective-permute-done.refs_0_ = bf16[16,7296]{1,0:T(8,128)(2,1)S(1)} collective-permute-done((bf16[16,7296]{1,0:T(8,128)(2,1)}, bf16[16,7296]{1,0:T(8,128)(2,1)S(1)}, u32[]{:S(2)}, u32[]{:S(2)}) %collective-permute-start) | collective-permute-done | bytes 233504 | tf_op jit(solution)/shard_map/ppermute | solution.py:24
  36.6 1.5 %collective-permute-start.9 = (bf16[16,7296]{1,0:T(8,128)(2,1)S(1)}, bf16[16,7296]{1,0:T(8,128)(2,1)S(1)}, u32[]{:S(2)}, u32[]{:S(2)}) collective-permute-start(bf16[16,7296]{1,0:T(8,128)(2,1)S(1)} %collective-permute-done.refs_0_), channel_id=1, source_target_pairs={{0,2},{1,3},{2,0},{3,1},{4,6},{5,7},{6,4},{7,5},{8,10},{9,11},{10,... | collective-permute-start | bytes 700424 | tf_op jit(solution)/shard_map/ppermute | solution.py:24
  38.2 0.5 collective-permute-start.1
  38.7 4.5 %collective-permute-done.9.refs_2_ = bf16[16,7296]{1,0:T(8,128)(2,1)S(1)} collective-permute-done((bf16[16,7296]{1,0:T(8,128)(2,1)S(1)}, bf16[16,7296]{1,0:T(8,128)(2,1)S(1)}, u32[]{:S(2)}, u32[]{:S(2)}) %collective-permute-start.9) | collective-permute-done | bytes 233504 | tf_op jit(solution)/shard_map/ppermute | solution.py:24
  43.2 1.5 %collective-permute-done.10.refs_3_ = bf16[16,7296]{1,0:T(8,128)(2,1)S(1)} collective-permute-done((bf16[16,7296]{1,0:T(8,128)(2,1)S(1)}, bf16[16,7296]{1,0:T(8,128)(2,1)S(1)}, u32[]{:S(2)}, u32[]{:S(2)}) %collective-permute-start.10) | collective-permute-done | bytes 233504 | tf_op jit(solution)/shard_map/ppermute | solution.py:24
  44.7 13.9 %expert.1 = (bf16[16,7168]{1,0:T(8,128)(2,1)S(1)}, bf16[16,7168]{1,0:T(8,128)(2,1)S(1)}, bf16[16,7168]{1,0:T(8,128)(2,1)S(1)}, bf16[16,7168]{1,0:T(8,128)(2,1)S(...) custom-call(s32[1]{0:T(128)} %bitcast.expert_ref, ...), custom_call_target="tpu_custom_call" | custom-call | flops 5637144576 | bytes 44040192 | tf_op jit(solution)/shard_map/expert/pallas_call | solution.py:216
  60.2 1.8 %collective-permute-start.19 = (bf16[16,7168]{1,0:T(8,128)(2,1)S(1)}, bf16[16,7168]{1,0:T(8,128)(2,1)S(1)}, u32[]{:S(2)}, u32[]{:S(2)}) collective-permute-start(bf16[16,7168]{1,0:T(8,128)(2,1)S(1)} %add.10), channel_id=1, source_target_pairs={{0,2},{1,3},{2,0},{3,1},{4,6},{5,7},{6,4},{7,5},{8,10},{9,11},{10,... | collective-permute-start | bytes 688136 | tf_op jit(solution)/shard_map/ppermute | solution.py:24
  62.0 0.5 collective-permute-start.16
  63.1 5.6 %collective-permute-done.19.refs_2_ = bf16[16,7168]{1,0:T(8,128)(2,1)S(1)} collective-permute-done((bf16[16,7168]{1,0:T(8,128)(2,1)S(1)}, bf16[16,7168]{1,0:T(8,128)(2,1)S(1)}, u32[]{:S(2)}, u32[]{:S(2)}) %collective-permute-start.19) | collective-permute-done | bytes 229408 | tf_op jit(solution)/shard_map/ppermute | solution.py:24
  68.7 1.7 %collective-permute-start.26 = (bf16[16,7168]{1,0:T(8,128)(2,1)S(1)}, bf16[16,7168]{1,0:T(8,128)(2,1)S(1)}, u32[]{:S(2)}, u32[]{:S(2)}) collective-permute-start(bf16[16,7168]{1,0:T(8,128)(2,1)S(1)} %add.14), channel_id=1, source_target_pairs={{0,2},{1,3},{2,0},{3,1},{4,6},{5,7},{6,4},{7,5},{8,10},{9,11},{10,... | collective-permute-start | bytes 688136 | tf_op jit(solution)/shard_map/ppermute | solution.py:24
  70.5 0.9 collective-permute-start.20
  71.5 2.2 %collective-permute-done.23.refs_2_ = bf16[16,7168]{1,0:T(8,128)(2,1)S(1)} collective-permute-done((bf16[16,7168]{1,0:T(8,128)(2,1)S(1)}, bf16[16,7168]{1,0:T(8,128)(2,1)S(1)}, u32[]{:S(2)}, u32[]{:S(2)}) %collective-permute-start.23) | collective-permute-done | bytes 229408 | tf_op jit(solution)/shard_map/ppermute | solution.py:24
  73.7 4.0 %collective-permute-done.26.refs_2_ = bf16[16,7168]{1,0:T(8,128)(2,1)S(1)} collective-permute-done((bf16[16,7168]{1,0:T(8,128)(2,1)S(1)}, bf16[16,7168]{1,0:T(8,128)(2,1)S(1)}, u32[]{:S(2)}, u32[]{:S(2)}) %collective-permute-start.26) | collective-permute-done | bytes 229408 | tf_op jit(solution)/shard_map/ppermute | solution.py:24
  77.8 0.6 collective-permute-done.20.refs_2_.refs_1_
  78.5 1.2 %collective-permute-start.27 = (bf16[16,7168]{1,0:T(8,128)(2,1)S(1)}, bf16[16,7168]{1,0:T(8,128)(2,1)S(1)}, u32[]{:S(2)}, u32[]{:S(2)}) collective-permute-start(bf16[16,7168]{1,0:T(8,128)(2,1)S(1)} %add.16), channel_id=1, source_target_pairs={{0,2},{1,3},{2,0},{3,1},{4,6},{5,7},{6,4},{7,5},{8,10},{9,11},{10,... | collective-permute-start | bytes 688136 | tf_op jit(solution)/shard_map/ppermute | solution.py:24
  79.7 0.9 collective-permute-start.28
  80.6 0.7 collective-permute-start.29
  81.3 3.5 %collective-permute-done.27.refs_2_ = bf16[16,7168]{1,0:T(8,128)(2,1)S(1)} collective-permute-done((bf16[16,7168]{1,0:T(8,128)(2,1)S(1)}, bf16[16,7168]{1,0:T(8,128)(2,1)S(1)}, u32[]{:S(2)}, u32[]{:S(2)}) %collective-permute-start.27) | collective-permute-done | bytes 229408 | tf_op jit(solution)/shard_map/ppermute | solution.py:24
  84.9 5.1 %collective-permute-done.28.refs_2_ = bf16[16,7168]{1,0:T(8,128)(2,1)S(1)} collective-permute-done((bf16[16,7168]{1,0:T(8,128)(2,1)S(1)}, bf16[16,7168]{1,0:T(8,128)(2,1)S(1)}, u32[]{:S(2)}, u32[]{:S(2)}) %collective-permute-start.28) | collective-permute-done | bytes 229408 | tf_op jit(solution)/shard_map/ppermute | solution.py:24
  90.0 2.1 %collective-permute-done.29.refs_3_ = bf16[16,7168]{1,0:T(8,128)(2,1)S(1)} collective-permute-done((bf16[16,7168]{1,0:T(8,128)(2,1)S(1)}, bf16[16,7168]{1,0:T(8,128)(2,1)S(1)}, u32[]{:S(2)}, u32[]{:S(2)}) %collective-permute-start.29) | collective-permute-done | bytes 229408 | tf_op jit(solution)/shard_map/ppermute | solution.py:24
  92.1 0.8 add.18
  (42 shorter events, 3.6 us)
Async XLA Ops:
  1.8 11.1 %collective-permute-start.2 = (bf16[16,7296]{1,0:T(8,128)(2,1)}, bf16[16,7296]{1,0:T(8,128)(2,1)S(1)}, u32[]{:S(2)}, u32[]{:S(2)}) collective-permute-start(bf16[16,7296]{1,0:T(8,128)(2,1)} %pack.1.refs_4_), channel_id=1, source_target_pairs={{0,12},{1,13},{2,14},{3,15},{4,8},{5,9},{6,10},{7,11},{8,4},{9,5},... | collective-permute-start | bytes 700424 | tf_op jit(solution)/shard_map/ppermute | solution.py:24
  6.9 12.7 %collective-permute-start.7 = (bf16[16,7296]{1,0:T(8,128)(2,1)}, bf16[16,7296]{1,0:T(8,128)(2,1)S(1)}, u32[]{:S(2)}, u32[]{:S(2)}) collective-permute-start(bf16[16,7296]{1,0:T(8,128)(2,1)} %pack.1.refs_4_), channel_id=1, source_target_pairs={{0,2},{1,3},{2,0},{3,1},{4,6},{5,7},{6,4},{7,5},{8,10},{9,11},{10,... | collective-permute-start | bytes 700424 | tf_op jit(solution)/shard_map/ppermute | solution.py:24
  12.9 6.8 %collective-permute-start.4 = (bf16[16,7296]{1,0:T(8,128)(2,1)S(1)}, bf16[16,7296]{1,0:T(8,128)(2,1)S(1)}, u32[]{:S(2)}, u32[]{:S(2)}) collective-permute-start(bf16[16,7296]{1,0:T(8,128)(2,1)S(1)} %collective-permute-done.2.refs_0_), channel_id=1, source_target_pairs={{0,2},{1,3},{2,0},{3,1},{4,6},{5,7},{6,4},{7,5},{8,10},{9,11},{10,... | collective-permute-start | bytes 700424 | tf_op jit(solution)/shard_map/ppermute | solution.py:24
  14.4 9.5 %collective-permute-start.11 = (bf16[16,7296]{1,0:T(8,128)(2,1)}, bf16[16,7296]{1,0:T(8,128)(2,1)S(1)}, u32[]{:S(2)}, u32[]{:S(2)}) collective-permute-start(bf16[16,7296]{1,0:T(8,128)(2,1)} %pack.1.refs_4_), channel_id=1, source_target_pairs={{0,4},{1,5},{2,6},{3,7},{4,0},{5,1},{6,2},{7,3},{8,12},{9,13},{10,... | collective-permute-start | bytes 700424 | tf_op jit(solution)/shard_map/ppermute | solution.py:24
  19.0 7.5 %collective-permute-start.6 = (bf16[16,7296]{1,0:T(8,128)(2,1)}, bf16[16,7296]{1,0:T(8,128)(2,1)S(1)}, u32[]{:S(2)}, u32[]{:S(2)}) collective-permute-start(bf16[16,7296]{1,0:T(8,128)(2,1)} %pack.1.refs_4_), channel_id=1, source_target_pairs={{0,1},{1,0},{2,3},{3,2},{4,5},{5,4},{6,7},{7,6},{8,9},{9,8},{10,11... | collective-permute-start | bytes 700424 | tf_op jit(solution)/shard_map/ppermute | solution.py:24
  19.0 8.0 %collective-permute-start.3 = (bf16[16,7296]{1,0:T(8,128)(2,1)S(1)}, bf16[16,7296]{1,0:T(8,128)(2,1)S(1)}, u32[]{:S(2)}, u32[]{:S(2)}) collective-permute-start(bf16[16,7296]{1,0:T(8,128)(2,1)S(1)} %collective-permute-done.2.refs_0_), channel_id=1, source_target_pairs={{0,1},{1,0},{2,3},{3,2},{4,5},{5,4},{6,7},{7,6},{8,9},{9,8},{10,11... | collective-permute-start | bytes 700424 | tf_op jit(solution)/shard_map/ppermute | solution.py:24
  19.5 7.5 %collective-permute-start.8 = (bf16[16,7296]{1,0:T(8,128)(2,1)S(1)}, bf16[16,7296]{1,0:T(8,128)(2,1)S(1)}, u32[]{:S(2)}, u32[]{:S(2)}) collective-permute-start(bf16[16,7296]{1,0:T(8,128)(2,1)S(1)} %collective-permute-done.7.refs_6_), channel_id=1, source_target_pairs={{0,1},{1,0},{2,3},{3,2},{4,5},{5,4},{6,7},{7,6},{8,9},{9,8},{10,11... | collective-permute-start | bytes 700424 | tf_op jit(solution)/shard_map/ppermute | solution.py:24
  19.7 7.3 %collective-permute-start.5 = (bf16[16,7296]{1,0:T(8,128)(2,1)S(1)}, bf16[16,7296]{1,0:T(8,128)(2,1)S(1)}, u32[]{:S(2)}, u32[]{:S(2)}) collective-permute-start(bf16[16,7296]{1,0:T(8,128)(2,1)S(1)} %collective-permute-done.4.refs_2_), channel_id=1, source_target_pairs={{0,1},{1,0},{2,3},{3,2},{4,5},{5,4},{6,7},{7,6},{8,9},{9,8},{10,11... | collective-permute-start | bytes 700424 | tf_op jit(solution)/shard_map/ppermute | solution.py:24
  23.9 12.7 %collective-permute-start = (bf16[16,7296]{1,0:T(8,128)(2,1)}, bf16[16,7296]{1,0:T(8,128)(2,1)S(1)}, u32[]{:S(2)}, u32[]{:S(2)}) collective-permute-start(bf16[16,7296]{1,0:T(8,128)(2,1)} %pack.1.refs_4_), channel_id=1, source_target_pairs={{0,8},{1,9},{2,10},{3,11},{4,12},{5,13},{6,14},{7,15},{8,0},{9,1},... | collective-permute-start | bytes 700424 | tf_op jit(solution)/shard_map/ppermute | solution.py:24
  26.5 12.2 %collective-permute-start.13 = (bf16[16,7296]{1,0:T(8,128)(2,1)S(1)}, bf16[16,7296]{1,0:T(8,128)(2,1)S(1)}, u32[]{:S(2)}, u32[]{:S(2)}) collective-permute-start(bf16[16,7296]{1,0:T(8,128)(2,1)S(1)} %collective-permute-done.11.refs_4_), channel_id=1, source_target_pairs={{0,2},{1,3},{2,0},{3,1},{4,6},{5,7},{6,4},{7,5},{8,10},{9,11},{10,... | collective-permute-start | bytes 700424 | tf_op jit(solution)/shard_map/ppermute | solution.py:24
  27.0 0.9 %copy-start = (bf16[16,7296]{1,0:T(8,128)(2,1)S(1)}, bf16[16,7296]{1,0:T(8,128)(2,1)}, u32[]{:S(2)}) copy-start(bf16[16,7296]{1,0:T(8,128)(2,1)} %pack.1.refs_4_) | copy-start | bytes 700420
  36.6 6.5 %collective-permute-start.9 = (bf16[16,7296]{1,0:T(8,128)(2,1)S(1)}, bf16[16,7296]{1,0:T(8,128)(2,1)S(1)}, u32[]{:S(2)}, u32[]{:S(2)}) collective-permute-start(bf16[16,7296]{1,0:T(8,128)(2,1)S(1)} %collective-permute-done.refs_0_), channel_id=1, source_target_pairs={{0,2},{1,3},{2,0},{3,1},{4,6},{5,7},{6,4},{7,5},{8,10},{9,11},{10,... | collective-permute-start | bytes 700424 | tf_op jit(solution)/shard_map/ppermute | solution.py:24
  38.1 5.0 %collective-permute-start.12 = (bf16[16,7296]{1,0:T(8,128)(2,1)S(1)}, bf16[16,7296]{1,0:T(8,128)(2,1)S(1)}, u32[]{:S(2)}, u32[]{:S(2)}) collective-permute-start(bf16[16,7296]{1,0:T(8,128)(2,1)S(1)} %collective-permute-done.11.refs_4_), channel_id=1, source_target_pairs={{0,1},{1,0},{2,3},{3,2},{4,5},{5,4},{6,7},{7,6},{8,9},{9,8},{10,11... | collective-permute-start | bytes 700424 | tf_op jit(solution)/shard_map/ppermute | solution.py:24
  38.2 5.0 %collective-permute-start.1 = (bf16[16,7296]{1,0:T(8,128)(2,1)S(1)}, bf16[16,7296]{1,0:T(8,128)(2,1)S(1)}, u32[]{:S(2)}, u32[]{:S(2)}) collective-permute-start(bf16[16,7296]{1,0:T(8,128)(2,1)S(1)} %collective-permute-done.refs_0_), channel_id=1, source_target_pairs={{0,1},{1,0},{2,3},{3,2},{4,5},{5,4},{6,7},{7,6},{8,9},{9,8},{10,11... | collective-permute-start | bytes 700424 | tf_op jit(solution)/shard_map/ppermute | solution.py:24
  38.7 4.5 %collective-permute-start.14 = (bf16[16,7296]{1,0:T(8,128)(2,1)S(1)}, bf16[16,7296]{1,0:T(8,128)(2,1)S(1)}, u32[]{:S(2)}, u32[]{:S(2)}) collective-permute-start(bf16[16,7296]{1,0:T(8,128)(2,1)S(1)} %collective-permute-done.13.refs_6_), channel_id=1, source_target_pairs={{0,1},{1,0},{2,3},{3,2},{4,5},{5,4},{6,7},{7,6},{8,9},{9,8},{10,11... | collective-permute-start | bytes 700424 | tf_op jit(solution)/shard_map/ppermute | solution.py:24
  43.2 1.5 %collective-permute-start.10 = (bf16[16,7296]{1,0:T(8,128)(2,1)S(1)}, bf16[16,7296]{1,0:T(8,128)(2,1)S(1)}, u32[]{:S(2)}, u32[]{:S(2)}) collective-permute-start(bf16[16,7296]{1,0:T(8,128)(2,1)S(1)} %collective-permute-done.9.refs_2_), channel_id=1, source_target_pairs={{0,1},{1,0},{2,3},{3,2},{4,5},{5,4},{6,7},{7,6},{8,9},{9,8},{10,11... | collective-permute-start | bytes 700424 | tf_op jit(solution)/shard_map/ppermute | solution.py:24
  58.6 1.6 %collective-permute-start.18 = (bf16[16,7168]{1,0:T(8,128)(2,1)S(1)}, bf16[16,7168]{1,0:T(8,128)(2,1)S(1)}, u32[]{:S(2)}, u32[]{:S(2)}) collective-permute-start(bf16[16,7168]{1,0:T(8,128)(2,1)S(1)} %get-tuple-element.38), channel_id=1, source_target_pairs={{0,1},{1,0},{2,3},{3,2},{4,5},{5,4},{6,7},{7,6},{8,9},{9,8},{10,11... | collective-permute-start | bytes 688136 | tf_op jit(solution)/shard_map/ppermute | solution.py:24
  58.8 3.2 %collective-permute-start.22 = (bf16[16,7168]{1,0:T(8,128)(2,1)S(1)}, bf16[16,7168]{1,0:T(8,128)(2,1)S(1)}, u32[]{:S(2)}, u32[]{:S(2)}) collective-permute-start(bf16[16,7168]{1,0:T(8,128)(2,1)S(1)} %get-tuple-element.42), channel_id=1, source_target_pairs={{0,1},{1,0},{2,3},{3,2},{4,5},{5,4},{6,7},{7,6},{8,9},{9,8},{10,11... | collective-permute-start | bytes 688136 | tf_op jit(solution)/shard_map/ppermute | solution.py:24
  59.2 3.4 %collective-permute-start.25 = (bf16[16,7168]{1,0:T(8,128)(2,1)S(1)}, bf16[16,7168]{1,0:T(8,128)(2,1)S(1)}, u32[]{:S(2)}, u32[]{:S(2)}) collective-permute-start(bf16[16,7168]{1,0:T(8,128)(2,1)S(1)} %get-tuple-element.46), channel_id=1, source_target_pairs={{0,1},{1,0},{2,3},{3,2},{4,5},{5,4},{6,7},{7,6},{8,9},{9,8},{10,11... | collective-permute-start | bytes 688136 | tf_op jit(solution)/shard_map/ppermute | solution.py:24
  59.3 3.7 %collective-permute-start.17 = (bf16[16,7168]{1,0:T(8,128)(2,1)S(1)}, bf16[16,7168]{1,0:T(8,128)(2,1)S(1)}, u32[]{:S(2)}, u32[]{:S(2)}) collective-permute-start(bf16[16,7168]{1,0:T(8,128)(2,1)S(1)} %get-tuple-element.36), channel_id=1, source_target_pairs={{0,1},{1,0},{2,3},{3,2},{4,5},{5,4},{6,7},{7,6},{8,9},{9,8},{10,11... | collective-permute-start | bytes 688136 | tf_op jit(solution)/shard_map/ppermute | solution.py:24
  60.2 8.5 %collective-permute-start.19 = (bf16[16,7168]{1,0:T(8,128)(2,1)S(1)}, bf16[16,7168]{1,0:T(8,128)(2,1)S(1)}, u32[]{:S(2)}, u32[]{:S(2)}) collective-permute-start(bf16[16,7168]{1,0:T(8,128)(2,1)S(1)} %add.10), channel_id=1, source_target_pairs={{0,2},{1,3},{2,0},{3,1},{4,6},{5,7},{6,4},{7,5},{8,10},{9,11},{10,... | collective-permute-start | bytes 688136 | tf_op jit(solution)/shard_map/ppermute | solution.py:24
  62.0 8.5 %collective-permute-start.21 = (bf16[16,7168]{1,0:T(8,128)(2,1)S(1)}, bf16[16,7168]{1,0:T(8,128)(2,1)S(1)}, u32[]{:S(2)}, u32[]{:S(2)}) collective-permute-start(bf16[16,7168]{1,0:T(8,128)(2,1)S(1)} %get-tuple-element.40), channel_id=1, source_target_pairs={{0,1},{1,0},{2,3},{3,2},{4,5},{5,4},{6,7},{7,6},{8,9},{9,8},{10,11... | collective-permute-start | bytes 688136 | tf_op jit(solution)/shard_map/ppermute | solution.py:24
  62.0 15.8 %collective-permute-start.16 = (bf16[16,7168]{1,0:T(8,128)(2,1)S(1)}, bf16[16,7168]{1,0:T(8,128)(2,1)S(1)}, u32[]{:S(2)}, u32[]{:S(2)}) collective-permute-start(bf16[16,7168]{1,0:T(8,128)(2,1)S(1)} %get-tuple-element.34), channel_id=1, source_target_pairs={{0,1},{1,0},{2,3},{3,2},{4,5},{5,4},{6,7},{7,6},{8,9},{9,8},{10,11... | collective-permute-start | bytes 688136 | tf_op jit(solution)/shard_map/ppermute | solution.py:24
  62.6 11.0 %collective-permute-start.23 = (bf16[16,7168]{1,0:T(8,128)(2,1)S(1)}, bf16[16,7168]{1,0:T(8,128)(2,1)S(1)}, u32[]{:S(2)}, u32[]{:S(2)}) collective-permute-start(bf16[16,7168]{1,0:T(8,128)(2,1)S(1)} %add.12), channel_id=1, source_target_pairs={{0,2},{1,3},{2,0},{3,1},{4,6},{5,7},{6,4},{7,5},{8,10},{9,11},{10,... | collective-permute-start | bytes 688136 | tf_op jit(solution)/shard_map/ppermute | solution.py:24
  63.0 10.7 %collective-permute-start.24 = (bf16[16,7168]{1,0:T(8,128)(2,1)S(1)}, bf16[16,7168]{1,0:T(8,128)(2,1)S(1)}, u32[]{:S(2)}, u32[]{:S(2)}) collective-permute-start(bf16[16,7168]{1,0:T(8,128)(2,1)S(1)} %get-tuple-element.44), channel_id=1, source_target_pairs={{0,1},{1,0},{2,3},{3,2},{4,5},{5,4},{6,7},{7,6},{8,9},{9,8},{10,11... | collective-permute-start | bytes 688136 | tf_op jit(solution)/shard_map/ppermute | solution.py:24
  68.7 9.0 %collective-permute-start.26 = (bf16[16,7168]{1,0:T(8,128)(2,1)S(1)}, bf16[16,7168]{1,0:T(8,128)(2,1)S(1)}, u32[]{:S(2)}, u32[]{:S(2)}) collective-permute-start(bf16[16,7168]{1,0:T(8,128)(2,1)S(1)} %add.14), channel_id=1, source_target_pairs={{0,2},{1,3},{2,0},{3,1},{4,6},{5,7},{6,4},{7,5},{8,10},{9,11},{10,... | collective-permute-start | bytes 688136 | tf_op jit(solution)/shard_map/ppermute | solution.py:24
  70.5 7.9 %collective-permute-start.20 = (bf16[16,7168]{1,0:T(8,128)(2,1)S(1)}, bf16[16,7168]{1,0:T(8,128)(2,1)S(1)}, u32[]{:S(2)}, u32[]{:S(2)}) collective-permute-start(bf16[16,7168]{1,0:T(8,128)(2,1)S(1)} %add.11.refs_3_), channel_id=1, source_target_pairs={{0,12},{1,13},{2,14},{3,15},{4,8},{5,9},{6,10},{7,11},{8,4},{9,5},... | collective-permute-start | bytes 688136 | tf_op jit(solution)/shard_map/ppermute | solution.py:24
  73.6 7.7 %collective-permute-start.15 = (bf16[16,7168]{1,0:T(8,128)(2,1)S(1)}, bf16[16,7168]{1,0:T(8,128)(2,1)S(1)}, u32[]{:S(2)}, u32[]{:S(2)}) collective-permute-start(bf16[16,7168]{1,0:T(8,128)(2,1)S(1)} %get-tuple-element.32), channel_id=1, source_target_pairs={{0,1},{1,0},{2,3},{3,2},{4,5},{5,4},{6,7},{7,6},{8,9},{9,8},{10,11... | collective-permute-start | bytes 688136 | tf_op jit(solution)/shard_map/ppermute | solution.py:24
  78.5 6.3 %collective-permute-start.27 = (bf16[16,7168]{1,0:T(8,128)(2,1)S(1)}, bf16[16,7168]{1,0:T(8,128)(2,1)S(1)}, u32[]{:S(2)}, u32[]{:S(2)}) collective-permute-start(bf16[16,7168]{1,0:T(8,128)(2,1)S(1)} %add.16), channel_id=1, source_target_pairs={{0,2},{1,3},{2,0},{3,1},{4,6},{5,7},{6,4},{7,5},{8,10},{9,11},{10,... | collective-permute-start | bytes 688136 | tf_op jit(solution)/shard_map/ppermute | solution.py:24
  79.7 10.3 %collective-permute-start.28 = (bf16[16,7168]{1,0:T(8,128)(2,1)S(1)}, bf16[16,7168]{1,0:T(8,128)(2,1)S(1)}, u32[]{:S(2)}, u32[]{:S(2)}) collective-permute-start(bf16[16,7168]{1,0:T(8,128)(2,1)S(1)} %add.13.refs_4_), channel_id=1, source_target_pairs={{0,4},{1,5},{2,6},{3,7},{4,0},{5,1},{6,2},{7,3},{8,12},{9,13},{10,... | collective-permute-start | bytes 688136 | tf_op jit(solution)/shard_map/ppermute | solution.py:24
  80.6 11.5 %collective-permute-start.29 = (bf16[16,7168]{1,0:T(8,128)(2,1)S(1)}, bf16[16,7168]{1,0:T(8,128)(2,1)S(1)}, u32[]{:S(2)}, u32[]{:S(2)}) collective-permute-start(bf16[16,7168]{1,0:T(8,128)(2,1)S(1)} %add.15.refs_5_), channel_id=1, source_target_pairs={{0,8},{1,9},{2,10},{3,11},{4,12},{5,13},{6,14},{7,15},{8,0},{9,1},... | collective-permute-start | bytes 688136 | tf_op jit(solution)/shard_map/ppermute | solution.py:24

commit v3 on v2

--- a/solution.py
+++ b/solution.py
@@ -294,7 +294,7 @@
     come = {k: pair(k) for k in turns}
     halves = {k: home(k, come[k], ()) for k in turns}
     came = {k: exchange(halves[k], k) for k in turns}
-    come[0] = pair(0, (came[first], *halves.values()))
+    come[0] = pair(0, (came[first],))
     return add([home(0, come[0], ()), *came.values()])
 
 

time: 93.1 us -> 92.3 us (level)
  waiting for transfers between devices: 39.7 us -> 37.9 us
  starting transfers between devices: 27.9 us -> 28.9 us
    ppermute x30, waiting for transfers between devices: 39.7 us -> 37.9 us  [exchange(): return lax.ppermute(x, 'local', [(i, i ^ distance) for i in range(n)])]
    ppermute x30, starting transfers between devices: 27.9 us -> 28.9 us  [exchange(): return lax.ppermute(x, 'local', [(i, i ^ distance) for i in range(n)])]
  transfers between devices with their start and end apart: 30 -> 30, of which waited for: 14 -> 12; matrix products, arithmetic and copies ran while one was open for 0% -> 0% of each run, Pallas kernels for 8% -> 8%
where the time goes in v3:
time: 92.3 us; the launch traced here: 92.1 us
  waiting for transfers between devices  37.9 us (41%)
  starting transfers between devices  28.9 us (31%)
  Pallas kernels  24.2 us (26%)
  local copies, waits for them, and re-layouts  0.93 us (1%)
    ppermute x30, waiting for transfers between devices, exchange(): return lax.ppermute(x, 'local', [(i, i ^ distance) for i in range(n)])  37.9 us
    ppermute x30, starting transfers between devices, exchange(): return lax.ppermute(x, 'local', [(i, i ^ distance) for i in range(n)])  28.9 us
    pallas_call x1, Pallas kernels, expert_part(): pl.pallas_call(functools.partial(expert_kernel, n), out_shape=[jax.ShapeD...  13.9 us
    pallas_call x1, Pallas kernels, early_part(): pl.pallas_call(functools.partial(early_kernel, n), out_shape=[jax.ShapeDt...  7.15 us
  transfers between devices with their start and end apart: 30, of which 12 were waited for; matrix products, arithmetic and copies ran while one was open for 0% of the time, Pallas kernels for 8%

profile of v3, /device:TPU:0, one launch (start us, length us, event | category | flops | bytes accessed | tf_op | source)
XLA Modules:
  0.0 92.1 jit_solution(14817940858631555050)
XLA Ops:
  0.0 1.8 %pack.1.refs_4_ = bf16[16,7296]{1,0:T(8,128)(2,1)} custom-call(bf16[16,7168]{1,0:T(8,128)(2,1)} %rows_ref.1, s32[4,16]{1,0:T(4,128)} %bitcast.3, s32[4,16]{1,0:T(4,128)} %bitcast.4), custom_call_target="tpu_custom_call" | custom-call | tf_op jit(solution)/shard_map/pack/pallas_call | solution.py:44
  1.8 5.0 %collective-permute-start.2 = (bf16[16,7296]{1,0:T(8,128)(2,1)}, bf16[16,7296]{1,0:T(8,128)(2,1)S(1)}, u32[]{:S(2)}, u32[]{:S(2)}) collective-permute-start(bf16[16,7296]{1,0:T(8,128)(2,1)} %pack.1.refs_4_), channel_id=1, source_target_pairs={{0,12},{1,13},{2,14},{3,15},{4,8},{5,9},{6,10},{7,11},{8,4},{9,5},... | collective-permute-start | bytes 700424 | tf_op jit(solution)/shard_map/ppermute | solution.py:24
  6.9 1.5 %collective-permute-start.7 = (bf16[16,7296]{1,0:T(8,128)(2,1)}, bf16[16,7296]{1,0:T(8,128)(2,1)S(1)}, u32[]{:S(2)}, u32[]{:S(2)}) collective-permute-start(bf16[16,7296]{1,0:T(8,128)(2,1)} %pack.1.refs_4_), channel_id=1, source_target_pairs={{0,2},{1,3},{2,0},{3,1},{4,6},{5,7},{6,4},{7,5},{8,10},{9,11},{10,... | collective-permute-start | bytes 700424 | tf_op jit(solution)/shard_map/ppermute | solution.py:24
  8.4 4.5 %collective-permute-done.2.refs_0_ = bf16[16,7296]{1,0:T(8,128)(2,1)S(1)} collective-permute-done((bf16[16,7296]{1,0:T(8,128)(2,1)}, bf16[16,7296]{1,0:T(8,128)(2,1)S(1)}, u32[]{:S(2)}, u32[]{:S(2)}) %collective-permute-start.2) | collective-permute-done | bytes 233504 | tf_op jit(solution)/shard_map/ppermute | solution.py:24
  12.9 1.5 %collective-permute-start.4 = (bf16[16,7296]{1,0:T(8,128)(2,1)S(1)}, bf16[16,7296]{1,0:T(8,128)(2,1)S(1)}, u32[]{:S(2)}, u32[]{:S(2)}) collective-permute-start(bf16[16,7296]{1,0:T(8,128)(2,1)S(1)} %collective-permute-done.2.refs_0_), channel_id=1, source_target_pairs={{0,2},{1,3},{2,0},{3,1},{4,6},{5,7},{6,4},{7,5},{8,10},{9,11},{10,... | collective-permute-start | bytes 700424 | tf_op jit(solution)/shard_map/ppermute | solution.py:24
  14.4 4.6 %collective-permute-start.11 = (bf16[16,7296]{1,0:T(8,128)(2,1)}, bf16[16,7296]{1,0:T(8,128)(2,1)S(1)}, u32[]{:S(2)}, u32[]{:S(2)}) collective-permute-start(bf16[16,7296]{1,0:T(8,128)(2,1)} %pack.1.refs_4_), channel_id=1, source_target_pairs={{0,4},{1,5},{2,6},{3,7},{4,0},{5,1},{6,2},{7,3},{8,12},{9,13},{10,... | collective-permute-start | bytes 700424 | tf_op jit(solution)/shard_map/ppermute | solution.py:24
  19.0 0.5 collective-permute-start.3
  20.0 3.9 %collective-permute-done.11.refs_4_ = bf16[16,7296]{1,0:T(8,128)(2,1)S(1)} collective-permute-done((bf16[16,7296]{1,0:T(8,128)(2,1)}, bf16[16,7296]{1,0:T(8,128)(2,1)S(1)}, u32[]{:S(2)}, u32[]{:S(2)}) %collective-permute-start.11) | collective-permute-done | bytes 233504 | tf_op jit(solution)/shard_map/ppermute | solution.py:24
  23.9 2.6 %collective-permute-start = (bf16[16,7296]{1,0:T(8,128)(2,1)}, bf16[16,7296]{1,0:T(8,128)(2,1)S(1)}, u32[]{:S(2)}, u32[]{:S(2)}) collective-permute-start(bf16[16,7296]{1,0:T(8,128)(2,1)} %pack.1.refs_4_), channel_id=1, source_target_pairs={{0,8},{1,9},{2,10},{3,11},{4,12},{5,13},{6,14},{7,15},{8,0},{9,1},... | collective-permute-start | bytes 700424 | tf_op jit(solution)/shard_map/ppermute | solution.py:24
  26.5 0.5 collective-permute-start.13
  27.0 0.9 %copy-done = bf16[16,7296]{1,0:T(8,128)(2,1)S(1)} copy-done((bf16[16,7296]{1,0:T(8,128)(2,1)S(1)}, bf16[16,7296]{1,0:T(8,128)(2,1)}, u32[]{:S(2)}) %copy-start) | copy-done | bytes 233496
  28.0 7.1 %early.1 = (bf16[64,7168]{1,0:T(8,128)(2,1)S(1)}, bf16[128,64]{1,0:T(8,128)(2,1)S(1)}, bf16[6,1024,1024]{2,1,0:T(8,128)(2,1)S(1)}) custom-call(s32[1]{0:T(128)} %bitcast.expert_ref, bf16[16,7296]{1,0:T(8,128)(2,1)S(1)} %collective-permute-done.2.refs_0_, bf16[16,7296]{1,0:T(8,128)(2,1)S(1)} %collective-permute-done.3.refs_1_, ...), custom_call_target="tpu_custom_call" | custom-call | flops 117440512 | bytes 12582912 | tf_op jit(solution)/shard_map/early/pallas_call | solution.py:129
  35.1 1.5 %collective-permute-done.refs_0_ = bf16[16,7296]{1,0:T(8,128)(2,1)S(1)} collective-permute-done((bf16[16,7296]{1,0:T(8,128)(2,1)}, bf16[16,7296]{1,0:T(8,128)(2,1)S(1)}, u32[]{:S(2)}, u32[]{:S(2)}) %collective-permute-start) | collective-permute-done | bytes 233504 | tf_op jit(solution)/shard_map/ppermute | solution.py:24
  36.6 1.5 %collective-permute-start.9 = (bf16[16,7296]{1,0:T(8,128)(2,1)S(1)}, bf16[16,7296]{1,0:T(8,128)(2,1)S(1)}, u32[]{:S(2)}, u32[]{:S(2)}) collective-permute-start(bf16[16,7296]{1,0:T(8,128)(2,1)S(1)} %collective-permute-done.refs_0_), channel_id=1, source_target_pairs={{0,2},{1,3},{2,0},{3,1},{4,6},{5,7},{6,4},{7,5},{8,10},{9,11},{10,... | collective-permute-start | bytes 700424 | tf_op jit(solution)/shard_map/ppermute | solution.py:24
  38.2 0.5 collective-permute-start.1
  38.7 4.5 %collective-permute-done.9.refs_2_ = bf16[16,7296]{1,0:T(8,128)(2,1)S(1)} collective-permute-done((bf16[16,7296]{1,0:T(8,128)(2,1)S(1)}, bf16[16,7296]{1,0:T(8,128)(2,1)S(1)}, u32[]{:S(2)}, u32[]{:S(2)}) %collective-permute-start.9) | collective-permute-done | bytes 233504 | tf_op jit(solution)/shard_map/ppermute | solution.py:24
  43.2 1.5 %collective-permute-done.10.refs_3_ = bf16[16,7296]{1,0:T(8,128)(2,1)S(1)} collective-permute-done((bf16[16,7296]{1,0:T(8,128)(2,1)S(1)}, bf16[16,7296]{1,0:T(8,128)(2,1)S(1)}, u32[]{:S(2)}, u32[]{:S(2)}) %collective-permute-start.10) | collective-permute-done | bytes 233504 | tf_op jit(solution)/shard_map/ppermute | solution.py:24
  44.7 13.9 %expert.1 = (bf16[16,7168]{1,0:T(8,128)(2,1)S(1)}, bf16[16,7168]{1,0:T(8,128)(2,1)S(1)}, bf16[16,7168]{1,0:T(8,128)(2,1)S(1)}, bf16[16,7168]{1,0:T(8,128)(2,1)S(...) custom-call(s32[1]{0:T(128)} %bitcast.expert_ref, ...), custom_call_target="tpu_custom_call" | custom-call | flops 5637144576 | bytes 44040192 | tf_op jit(solution)/shard_map/expert/pallas_call | solution.py:216
  58.8 0.4 collective-permute-start.23
  59.3 0.8 collective-permute-done.18.refs_1_
  60.2 1.8 %collective-permute-start.19 = (bf16[16,7168]{1,0:T(8,128)(2,1)S(1)}, bf16[16,7168]{1,0:T(8,128)(2,1)S(1)}, u32[]{:S(2)}, u32[]{:S(2)}) collective-permute-start(bf16[16,7168]{1,0:T(8,128)(2,1)S(1)} %add.10), channel_id=1, source_target_pairs={{0,2},{1,3},{2,0},{3,1},{4,6},{5,7},{6,4},{7,5},{8,10},{9,11},{10,... | collective-permute-start | bytes 688136 | tf_op jit(solution)/shard_map/ppermute | solution.py:24
  62.0 0.5 collective-permute-start.22
  62.9 5.8 %collective-permute-done.19.refs_2_ = bf16[16,7168]{1,0:T(8,128)(2,1)S(1)} collective-permute-done((bf16[16,7168]{1,0:T(8,128)(2,1)S(1)}, bf16[16,7168]{1,0:T(8,128)(2,1)S(1)}, u32[]{:S(2)}, u32[]{:S(2)}) %collective-permute-start.19) | collective-permute-done | bytes 229408 | tf_op jit(solution)/shard_map/ppermute | solution.py:24
  68.8 1.1 %collective-permute-start.20 = (bf16[16,7168]{1,0:T(8,128)(2,1)S(1)}, bf16[16,7168]{1,0:T(8,128)(2,1)S(1)}, u32[]{:S(2)}, u32[]{:S(2)}) collective-permute-start(bf16[16,7168]{1,0:T(8,128)(2,1)S(1)} %add.11), channel_id=1, source_target_pairs={{0,12},{1,13},{2,14},{3,15},{4,8},{5,9},{6,10},{7,11},{8,4},{9,5},... | collective-permute-start | bytes 688136 | tf_op jit(solution)/shard_map/ppermute | solution.py:24
  70.0 1.6 %collective-permute-start.28 = (bf16[16,7168]{1,0:T(8,128)(2,1)S(1)}, bf16[16,7168]{1,0:T(8,128)(2,1)S(1)}, u32[]{:S(2)}, u32[]{:S(2)}) collective-permute-start(bf16[16,7168]{1,0:T(8,128)(2,1)S(1)} %add.16), channel_id=1, source_target_pairs={{0,2},{1,3},{2,0},{3,1},{4,6},{5,7},{6,4},{7,5},{8,10},{9,11},{10,... | collective-permute-start | bytes 688136 | tf_op jit(solution)/shard_map/ppermute | solution.py:24
  71.6 1.2 %collective-permute-done.24.refs_2_ = bf16[16,7168]{1,0:T(8,128)(2,1)S(1)} collective-permute-done((bf16[16,7168]{1,0:T(8,128)(2,1)S(1)}, bf16[16,7168]{1,0:T(8,128)(2,1)S(1)}, u32[]{:S(2)}, u32[]{:S(2)}) %collective-permute-start.24) | collective-permute-done | bytes 229408 | tf_op jit(solution)/shard_map/ppermute | solution.py:24
  73.0 4.3 %collective-permute-done.20.refs_2_.refs_1_ = bf16[16,7168]{1,0:T(8,128)(2,1)S(1)} collective-permute-done((bf16[16,7168]{1,0:T(8,128)(2,1)S(1)}, bf16[16,7168]{1,0:T(8,128)(2,1)S(1)}, u32[]{:S(2)}, u32[]{:S(2)}) %collective-permute-start.20) | collective-permute-done | bytes 229408 | tf_op jit(solution)/shard_map/ppermute | solution.py:24
  77.3 2.2 %collective-permute-start.21 = (bf16[16,7168]{1,0:T(8,128)(2,1)S(1)}, bf16[16,7168]{1,0:T(8,128)(2,1)S(1)}, u32[]{:S(2)}, u32[]{:S(2)}) collective-permute-start(bf16[16,7168]{1,0:T(8,128)(2,1)S(1)} %add.12), channel_id=1, source_target_pairs={{0,2},{1,3},{2,0},{3,1},{4,6},{5,7},{6,4},{7,5},{8,10},{9,11},{10,... | collective-permute-start | bytes 688136 | tf_op jit(solution)/shard_map/ppermute | solution.py:24
  79.6 1.8 %collective-permute-start.29 = (bf16[16,7168]{1,0:T(8,128)(2,1)S(1)}, bf16[16,7168]{1,0:T(8,128)(2,1)S(1)}, u32[]{:S(2)}, u32[]{:S(2)}) collective-permute-start(bf16[16,7168]{1,0:T(8,128)(2,1)S(1)} %add.17), channel_id=1, source_target_pairs={{0,8},{1,9},{2,10},{3,11},{4,12},{5,13},{6,14},{7,15},{8,0},{9,1},... | collective-permute-start | bytes 688136 | tf_op jit(solution)/shard_map/ppermute | solution.py:24
  81.5 2.1 %collective-permute-done.21.refs_2_ = bf16[16,7168]{1,0:T(8,128)(2,1)S(1)} collective-permute-done((bf16[16,7168]{1,0:T(8,128)(2,1)S(1)}, bf16[16,7168]{1,0:T(8,128)(2,1)S(1)}, u32[]{:S(2)}, u32[]{:S(2)}) %collective-permute-start.21) | collective-permute-done | bytes 229408 | tf_op jit(solution)/shard_map/ppermute | solution.py:24
  83.6 7.7 %collective-permute-done.29.refs_3_ = bf16[16,7168]{1,0:T(8,128)(2,1)S(1)} collective-permute-done((bf16[16,7168]{1,0:T(8,128)(2,1)S(1)}, bf16[16,7168]{1,0:T(8,128)(2,1)S(1)}, u32[]{:S(2)}, u32[]{:S(2)}) %collective-permute-start.29) | collective-permute-done | bytes 229408 | tf_op jit(solution)/shard_map/ppermute | solution.py:24
  91.3 0.8 add.18
  (42 shorter events, 1.9 us)
Async XLA Ops:
  1.8 11.1 %collective-permute-start.2 = (bf16[16,7296]{1,0:T(8,128)(2,1)}, bf16[16,7296]{1,0:T(8,128)(2,1)S(1)}, u32[]{:S(2)}, u32[]{:S(2)}) collective-permute-start(bf16[16,7296]{1,0:T(8,128)(2,1)} %pack.1.refs_4_), channel_id=1, source_target_pairs={{0,12},{1,13},{2,14},{3,15},{4,8},{5,9},{6,10},{7,11},{8,4},{9,5},... | collective-permute-start | bytes 700424 | tf_op jit(solution)/shard_map/ppermute | solution.py:24
  6.9 12.7 %collective-permute-start.7 = (bf16[16,7296]{1,0:T(8,128)(2,1)}, bf16[16,7296]{1,0:T(8,128)(2,1)S(1)}, u32[]{:S(2)}, u32[]{:S(2)}) collective-permute-start(bf16[16,7296]{1,0:T(8,128)(2,1)} %pack.1.refs_4_), channel_id=1, source_target_pairs={{0,2},{1,3},{2,0},{3,1},{4,6},{5,7},{6,4},{7,5},{8,10},{9,11},{10,... | collective-permute-start | bytes 700424 | tf_op jit(solution)/shard_map/ppermute | solution.py:24
  12.9 6.8 %collective-permute-start.4 = (bf16[16,7296]{1,0:T(8,128)(2,1)S(1)}, bf16[16,7296]{1,0:T(8,128)(2,1)S(1)}, u32[]{:S(2)}, u32[]{:S(2)}) collective-permute-start(bf16[16,7296]{1,0:T(8,128)(2,1)S(1)} %collective-permute-done.2.refs_0_), channel_id=1, source_target_pairs={{0,2},{1,3},{2,0},{3,1},{4,6},{5,7},{6,4},{7,5},{8,10},{9,11},{10,... | collective-permute-start | bytes 700424 | tf_op jit(solution)/shard_map/ppermute | solution.py:24
  14.4 9.5 %collective-permute-start.11 = (bf16[16,7296]{1,0:T(8,128)(2,1)}, bf16[16,7296]{1,0:T(8,128)(2,1)S(1)}, u32[]{:S(2)}, u32[]{:S(2)}) collective-permute-start(bf16[16,7296]{1,0:T(8,128)(2,1)} %pack.1.refs_4_), channel_id=1, source_target_pairs={{0,4},{1,5},{2,6},{3,7},{4,0},{5,1},{6,2},{7,3},{8,12},{9,13},{10,... | collective-permute-start | bytes 700424 | tf_op jit(solution)/shard_map/ppermute | solution.py:24
  19.0 7.5 %collective-permute-start.6 = (bf16[16,7296]{1,0:T(8,128)(2,1)}, bf16[16,7296]{1,0:T(8,128)(2,1)S(1)}, u32[]{:S(2)}, u32[]{:S(2)}) collective-permute-start(bf16[16,7296]{1,0:T(8,128)(2,1)} %pack.1.refs_4_), channel_id=1, source_target_pairs={{0,1},{1,0},{2,3},{3,2},{4,5},{5,4},{6,7},{7,6},{8,9},{9,8},{10,11... | collective-permute-start | bytes 700424 | tf_op jit(solution)/shard_map/ppermute | solution.py:24
  19.0 8.0 %collective-permute-start.3 = (bf16[16,7296]{1,0:T(8,128)(2,1)S(1)}, bf16[16,7296]{1,0:T(8,128)(2,1)S(1)}, u32[]{:S(2)}, u32[]{:S(2)}) collective-permute-start(bf16[16,7296]{1,0:T(8,128)(2,1)S(1)} %collective-permute-done.2.refs_0_), channel_id=1, source_target_pairs={{0,1},{1,0},{2,3},{3,2},{4,5},{5,4},{6,7},{7,6},{8,9},{9,8},{10,11... | collective-permute-start | bytes 700424 | tf_op jit(solution)/shard_map/ppermute | solution.py:24
  19.5 7.5 %collective-permute-start.8 = (bf16[16,7296]{1,0:T(8,128)(2,1)S(1)}, bf16[16,7296]{1,0:T(8,128)(2,1)S(1)}, u32[]{:S(2)}, u32[]{:S(2)}) collective-permute-start(bf16[16,7296]{1,0:T(8,128)(2,1)S(1)} %collective-permute-done.7.refs_6_), channel_id=1, source_target_pairs={{0,1},{1,0},{2,3},{3,2},{4,5},{5,4},{6,7},{7,6},{8,9},{9,8},{10,11... | collective-permute-start | bytes 700424 | tf_op jit(solution)/shard_map/ppermute | solution.py:24
  19.7 7.3 %collective-permute-start.5 = (bf16[16,7296]{1,0:T(8,128)(2,1)S(1)}, bf16[16,7296]{1,0:T(8,128)(2,1)S(1)}, u32[]{:S(2)}, u32[]{:S(2)}) collective-permute-start(bf16[16,7296]{1,0:T(8,128)(2,1)S(1)} %collective-permute-done.4.refs_2_), channel_id=1, source_target_pairs={{0,1},{1,0},{2,3},{3,2},{4,5},{5,4},{6,7},{7,6},{8,9},{9,8},{10,11... | collective-permute-start | bytes 700424 | tf_op jit(solution)/shard_map/ppermute | solution.py:24
  23.9 12.7 %collective-permute-start = (bf16[16,7296]{1,0:T(8,128)(2,1)}, bf16[16,7296]{1,0:T(8,128)(2,1)S(1)}, u32[]{:S(2)}, u32[]{:S(2)}) collective-permute-start(bf16[16,7296]{1,0:T(8,128)(2,1)} %pack.1.refs_4_), channel_id=1, source_target_pairs={{0,8},{1,9},{2,10},{3,11},{4,12},{5,13},{6,14},{7,15},{8,0},{9,1},... | collective-permute-start | bytes 700424 | tf_op jit(solution)/shard_map/ppermute | solution.py:24
  26.5 12.2 %collective-permute-start.13 = (bf16[16,7296]{1,0:T(8,128)(2,1)S(1)}, bf16[16,7296]{1,0:T(8,128)(2,1)S(1)}, u32[]{:S(2)}, u32[]{:S(2)}) collective-permute-start(bf16[16,7296]{1,0:T(8,128)(2,1)S(1)} %collective-permute-done.11.refs_4_), channel_id=1, source_target_pairs={{0,2},{1,3},{2,0},{3,1},{4,6},{5,7},{6,4},{7,5},{8,10},{9,11},{10,... | collective-permute-start | bytes 700424 | tf_op jit(solution)/shard_map/ppermute | solution.py:24
  27.0 0.9 %copy-start = (bf16[16,7296]{1,0:T(8,128)(2,1)S(1)}, bf16[16,7296]{1,0:T(8,128)(2,1)}, u32[]{:S(2)}) copy-start(bf16[16,7296]{1,0:T(8,128)(2,1)} %pack.1.refs_4_) | copy-start | bytes 700420
  36.6 6.5 %collective-permute-start.9 = (bf16[16,7296]{1,0:T(8,128)(2,1)S(1)}, bf16[16,7296]{1,0:T(8,128)(2,1)S(1)}, u32[]{:S(2)}, u32[]{:S(2)}) collective-permute-start(bf16[16,7296]{1,0:T(8,128)(2,1)S(1)} %collective-permute-done.refs_0_), channel_id=1, source_target_pairs={{0,2},{1,3},{2,0},{3,1},{4,6},{5,7},{6,4},{7,5},{8,10},{9,11},{10,... | collective-permute-start | bytes 700424 | tf_op jit(solution)/shard_map/ppermute | solution.py:24
  38.1 5.0 %collective-permute-start.12 = (bf16[16,7296]{1,0:T(8,128)(2,1)S(1)}, bf16[16,7296]{1,0:T(8,128)(2,1)S(1)}, u32[]{:S(2)}, u32[]{:S(2)}) collective-permute-start(bf16[16,7296]{1,0:T(8,128)(2,1)S(1)} %collective-permute-done.11.refs_4_), channel_id=1, source_target_pairs={{0,1},{1,0},{2,3},{3,2},{4,5},{5,4},{6,7},{7,6},{8,9},{9,8},{10,11... | collective-permute-start | bytes 700424 | tf_op jit(solution)/shard_map/ppermute | solution.py:24
  38.2 5.0 %collective-permute-start.1 = (bf16[16,7296]{1,0:T(8,128)(2,1)S(1)}, bf16[16,7296]{1,0:T(8,128)(2,1)S(1)}, u32[]{:S(2)}, u32[]{:S(2)}) collective-permute-start(bf16[16,7296]{1,0:T(8,128)(2,1)S(1)} %collective-permute-done.refs_0_), channel_id=1, source_target_pairs={{0,1},{1,0},{2,3},{3,2},{4,5},{5,4},{6,7},{7,6},{8,9},{9,8},{10,11... | collective-permute-start | bytes 700424 | tf_op jit(solution)/shard_map/ppermute | solution.py:24
  38.7 4.5 %collective-permute-start.14 = (bf16[16,7296]{1,0:T(8,128)(2,1)S(1)}, bf16[16,7296]{1,0:T(8,128)(2,1)S(1)}, u32[]{:S(2)}, u32[]{:S(2)}) collective-permute-start(bf16[16,7296]{1,0:T(8,128)(2,1)S(1)} %collective-permute-done.13.refs_6_), channel_id=1, source_target_pairs={{0,1},{1,0},{2,3},{3,2},{4,5},{5,4},{6,7},{7,6},{8,9},{9,8},{10,11... | collective-permute-start | bytes 700424 | tf_op jit(solution)/shard_map/ppermute | solution.py:24
  43.2 1.5 %collective-permute-start.10 = (bf16[16,7296]{1,0:T(8,128)(2,1)S(1)}, bf16[16,7296]{1,0:T(8,128)(2,1)S(1)}, u32[]{:S(2)}, u32[]{:S(2)}) collective-permute-start(bf16[16,7296]{1,0:T(8,128)(2,1)S(1)} %collective-permute-done.9.refs_2_), channel_id=1, source_target_pairs={{0,1},{1,0},{2,3},{3,2},{4,5},{5,4},{6,7},{7,6},{8,9},{9,8},{10,11... | collective-permute-start | bytes 700424 | tf_op jit(solution)/shard_map/ppermute | solution.py:24
  58.6 1.6 %collective-permute-start.18 = (bf16[16,7168]{1,0:T(8,128)(2,1)S(1)}, bf16[16,7168]{1,0:T(8,128)(2,1)S(1)}, u32[]{:S(2)}, u32[]{:S(2)}) collective-permute-start(bf16[16,7168]{1,0:T(8,128)(2,1)S(1)} %get-tuple-element.38), channel_id=1, source_target_pairs={{0,1},{1,0},{2,3},{3,2},{4,5},{5,4},{6,7},{7,6},{8,9},{9,8},{10,11... | collective-permute-start | bytes 688136 | tf_op jit(solution)/shard_map/ppermute | solution.py:24
  58.8 3.7 %collective-permute-start.23 = (bf16[16,7168]{1,0:T(8,128)(2,1)S(1)}, bf16[16,7168]{1,0:T(8,128)(2,1)S(1)}, u32[]{:S(2)}, u32[]{:S(2)}) collective-permute-start(bf16[16,7168]{1,0:T(8,128)(2,1)S(1)} %get-tuple-element.42), channel_id=1, source_target_pairs={{0,1},{1,0},{2,3},{3,2},{4,5},{5,4},{6,7},{7,6},{8,9},{9,8},{10,11... | collective-permute-start | bytes 688136 | tf_op jit(solution)/shard_map/ppermute | solution.py:24
  59.2 3.8 %collective-permute-start.17 = (bf16[16,7168]{1,0:T(8,128)(2,1)S(1)}, bf16[16,7168]{1,0:T(8,128)(2,1)S(1)}, u32[]{:S(2)}, u32[]{:S(2)}) collective-permute-start(bf16[16,7168]{1,0:T(8,128)(2,1)S(1)} %get-tuple-element.36), channel_id=1, source_target_pairs={{0,1},{1,0},{2,3},{3,2},{4,5},{5,4},{6,7},{7,6},{8,9},{9,8},{10,11... | collective-permute-start | bytes 688136 | tf_op jit(solution)/shard_map/ppermute | solution.py:24
  60.2 8.5 %collective-permute-start.19 = (bf16[16,7168]{1,0:T(8,128)(2,1)S(1)}, bf16[16,7168]{1,0:T(8,128)(2,1)S(1)}, u32[]{:S(2)}, u32[]{:S(2)}) collective-permute-start(bf16[16,7168]{1,0:T(8,128)(2,1)S(1)} %add.10), channel_id=1, source_target_pairs={{0,2},{1,3},{2,0},{3,1},{4,6},{5,7},{6,4},{7,5},{8,10},{9,11},{10,... | collective-permute-start | bytes 688136 | tf_op jit(solution)/shard_map/ppermute | solution.py:24
  62.0 7.9 %collective-permute-start.27 = (bf16[16,7168]{1,0:T(8,128)(2,1)S(1)}, bf16[16,7168]{1,0:T(8,128)(2,1)S(1)}, u32[]{:S(2)}, u32[]{:S(2)}) collective-permute-start(bf16[16,7168]{1,0:T(8,128)(2,1)S(1)} %get-tuple-element.46), channel_id=1, source_target_pairs={{0,1},{1,0},{2,3},{3,2},{4,5},{5,4},{6,7},{7,6},{8,9},{9,8},{10,11... | collective-permute-start | bytes 688136 | tf_op jit(solution)/shard_map/ppermute | solution.py:24
  62.0 8.0 %collective-permute-start.22 = (bf16[16,7168]{1,0:T(8,128)(2,1)S(1)}, bf16[16,7168]{1,0:T(8,128)(2,1)S(1)}, u32[]{:S(2)}, u32[]{:S(2)}) collective-permute-start(bf16[16,7168]{1,0:T(8,128)(2,1)S(1)} %get-tuple-element.40), channel_id=1, source_target_pairs={{0,1},{1,0},{2,3},{3,2},{4,5},{5,4},{6,7},{7,6},{8,9},{9,8},{10,11... | collective-permute-start | bytes 688136 | tf_op jit(solution)/shard_map/ppermute | solution.py:24
  62.6 10.3 %collective-permute-start.24 = (bf16[16,7168]{1,0:T(8,128)(2,1)S(1)}, bf16[16,7168]{1,0:T(8,128)(2,1)S(1)}, u32[]{:S(2)}, u32[]{:S(2)}) collective-permute-start(bf16[16,7168]{1,0:T(8,128)(2,1)S(1)} %add.14), channel_id=1, source_target_pairs={{0,2},{1,3},{2,0},{3,1},{4,6},{5,7},{6,4},{7,5},{8,10},{9,11},{10,... | collective-permute-start | bytes 688136 | tf_op jit(solution)/shard_map/ppermute | solution.py:24
  62.9 10.0 %collective-permute-start.16 = (bf16[16,7168]{1,0:T(8,128)(2,1)S(1)}, bf16[16,7168]{1,0:T(8,128)(2,1)S(1)}, u32[]{:S(2)}, u32[]{:S(2)}) collective-permute-start(bf16[16,7168]{1,0:T(8,128)(2,1)S(1)} %get-tuple-element.34), channel_id=1, source_target_pairs={{0,1},{1,0},{2,3},{3,2},{4,5},{5,4},{6,7},{7,6},{8,9},{9,8},{10,11... | collective-permute-start | bytes 688136 | tf_op jit(solution)/shard_map/ppermute | solution.py:24
  68.8 8.5 %collective-permute-start.20 = (bf16[16,7168]{1,0:T(8,128)(2,1)S(1)}, bf16[16,7168]{1,0:T(8,128)(2,1)S(1)}, u32[]{:S(2)}, u32[]{:S(2)}) collective-permute-start(bf16[16,7168]{1,0:T(8,128)(2,1)S(1)} %add.11), channel_id=1, source_target_pairs={{0,12},{1,13},{2,14},{3,15},{4,8},{5,9},{6,10},{7,11},{8,4},{9,5},... | collective-permute-start | bytes 688136 | tf_op jit(solution)/shard_map/ppermute | solution.py:24
  69.9 9.6 %collective-permute-start.26 = (bf16[16,7168]{1,0:T(8,128)(2,1)S(1)}, bf16[16,7168]{1,0:T(8,128)(2,1)S(1)}, u32[]{:S(2)}, u32[]{:S(2)}) collective-permute-start(bf16[16,7168]{1,0:T(8,128)(2,1)S(1)} %get-tuple-element.44), channel_id=1, source_target_pairs={{0,1},{1,0},{2,3},{3,2},{4,5},{5,4},{6,7},{7,6},{8,9},{9,8},{10,11... | collective-permute-start | bytes 688136 | tf_op jit(solution)/shard_map/ppermute | solution.py:24
  70.0 9.5 %collective-permute-start.28 = (bf16[16,7168]{1,0:T(8,128)(2,1)S(1)}, bf16[16,7168]{1,0:T(8,128)(2,1)S(1)}, u32[]{:S(2)}, u32[]{:S(2)}) collective-permute-start(bf16[16,7168]{1,0:T(8,128)(2,1)S(1)} %add.16), channel_id=1, source_target_pairs={{0,2},{1,3},{2,0},{3,1},{4,6},{5,7},{6,4},{7,5},{8,10},{9,11},{10,... | collective-permute-start | bytes 688136 | tf_op jit(solution)/shard_map/ppermute | solution.py:24
  72.8 8.7 %collective-permute-start.15 = (bf16[16,7168]{1,0:T(8,128)(2,1)S(1)}, bf16[16,7168]{1,0:T(8,128)(2,1)S(1)}, u32[]{:S(2)}, u32[]{:S(2)}) collective-permute-start(bf16[16,7168]{1,0:T(8,128)(2,1)S(1)} %get-tuple-element.32), channel_id=1, source_target_pairs={{0,1},{1,0},{2,3},{3,2},{4,5},{5,4},{6,7},{7,6},{8,9},{9,8},{10,11... | collective-permute-start | bytes 688136 | tf_op jit(solution)/shard_map/ppermute | solution.py:24
  72.9 10.7 %collective-permute-start.25 = (bf16[16,7168]{1,0:T(8,128)(2,1)S(1)}, bf16[16,7168]{1,0:T(8,128)(2,1)S(1)}, u32[]{:S(2)}, u32[]{:S(2)}) collective-permute-start(bf16[16,7168]{1,0:T(8,128)(2,1)S(1)} %add.15), channel_id=1, source_target_pairs={{0,4},{1,5},{2,6},{3,7},{4,0},{5,1},{6,2},{7,3},{8,12},{9,13},{10,... | collective-permute-start | bytes 688136 | tf_op jit(solution)/shard_map/ppermute | solution.py:24
  77.3 6.2 %collective-permute-start.21 = (bf16[16,7168]{1,0:T(8,128)(2,1)S(1)}, bf16[16,7168]{1,0:T(8,128)(2,1)S(1)}, u32[]{:S(2)}, u32[]{:S(2)}) collective-permute-start(bf16[16,7168]{1,0:T(8,128)(2,1)S(1)} %add.12), channel_id=1, source_target_pairs={{0,2},{1,3},{2,0},{3,1},{4,6},{5,7},{6,4},{7,5},{8,10},{9,11},{10,... | collective-permute-start | bytes 688136 | tf_op jit(solution)/shard_map/ppermute | solution.py:24
  79.6 11.7 %collective-permute-start.29 = (bf16[16,7168]{1,0:T(8,128)(2,1)S(1)}, bf16[16,7168]{1,0:T(8,128)(2,1)S(1)}, u32[]{:S(2)}, u32[]{:S(2)}) collective-permute-start(bf16[16,7168]{1,0:T(8,128)(2,1)S(1)} %add.17), channel_id=1, source_target_pairs={{0,8},{1,9},{2,10},{3,11},{4,12},{5,13},{6,14},{7,15},{8,0},{9,1},... | collective-permute-start | bytes 688136 | tf_op jit(solution)/shard_map/ppermute | solution.py:24

commit v4 on v3

--- a/solution.py
+++ b/solution.py
@@ -11,7 +11,7 @@
 CAP = 8
 LANES = 128
 RING = 7
-EARLY = 6
+EARLY = 8
 denominator = 64.0
 VMEM = pl.BlockSpec(memory_space=pltpu.VMEM)
 SMEM = pl.BlockSpec(memory_space=pltpu.SMEM)

time: 92.3 us -> 91.9 us (level)
    pallas_call x1, Pallas kernels: 7.15 us -> 8.36 us  [early_part(): pl.pallas_call(functools.partial(early_kernel, n), out_shape=[jax.ShapeDt...]
    pallas_call x1, Pallas kernels: 13.9 us -> 13 us  [expert_part(): pl.pallas_call(functools.partial(expert_kernel, n), out_shape=[jax.ShapeD...]
  transfers between devices with their start and end apart: 30 -> 30, of which waited for: 12 -> 12; matrix products, arithmetic and copies ran while one was open for 0% -> 0% of each run, Pallas kernels for 8% -> 10%
where the time goes in v4:
time: 91.9 us; the launch traced here: 91.7 us
  waiting for transfers between devices  37.6 us (41%)
  starting transfers between devices  28.6 us (31%)
  Pallas kernels  24.5 us (27%)
  local copies, waits for them, and re-layouts  0.93 us (1%)
    ppermute x30, waiting for transfers between devices, exchange(): return lax.ppermute(x, 'local', [(i, i ^ distance) for i in range(n)])  37.6 us
    ppermute x30, starting transfers between devices, exchange(): return lax.ppermute(x, 'local', [(i, i ^ distance) for i in range(n)])  28.6 us
    pallas_call x1, Pallas kernels, expert_part(): pl.pallas_call(functools.partial(expert_kernel, n), out_shape=[jax.ShapeD...  13 us
    pallas_call x1, Pallas kernels, early_part(): pl.pallas_call(functools.partial(early_kernel, n), out_shape=[jax.ShapeDt...  8.36 us
  transfers between devices with their start and end apart: 30, of which 12 were waited for; matrix products, arithmetic and copies ran while one was open for 0% of the time, Pallas kernels for 10%

profile of v4, /device:TPU:0, one launch (start us, length us, event | category | flops | bytes accessed | tf_op | source)
XLA Modules:
  0.0 91.7 jit_solution(6535522776100131415)
XLA Ops:
  0.0 1.8 %pack.1.refs_4_ = bf16[16,7296]{1,0:T(8,128)(2,1)} custom-call(bf16[16,7168]{1,0:T(8,128)(2,1)} %rows_ref.1, s32[4,16]{1,0:T(4,128)} %bitcast.3, s32[4,16]{1,0:T(4,128)} %bitcast.4), custom_call_target="tpu_custom_call" | custom-call | tf_op jit(solution)/shard_map/pack/pallas_call | solution.py:44
  1.8 5.0 %collective-permute-start.2 = (bf16[16,7296]{1,0:T(8,128)(2,1)}, bf16[16,7296]{1,0:T(8,128)(2,1)S(1)}, u32[]{:S(2)}, u32[]{:S(2)}) collective-permute-start(bf16[16,7296]{1,0:T(8,128)(2,1)} %pack.1.refs_4_), channel_id=1, source_target_pairs={{0,12},{1,13},{2,14},{3,15},{4,8},{5,9},{6,10},{7,11},{8,4},{9,5},... | collective-permute-start | bytes 700424 | tf_op jit(solution)/shard_map/ppermute | solution.py:24
  6.9 1.5 %collective-permute-start.7 = (bf16[16,7296]{1,0:T(8,128)(2,1)}, bf16[16,7296]{1,0:T(8,128)(2,1)S(1)}, u32[]{:S(2)}, u32[]{:S(2)}) collective-permute-start(bf16[16,7296]{1,0:T(8,128)(2,1)} %pack.1.refs_4_), channel_id=1, source_target_pairs={{0,2},{1,3},{2,0},{3,1},{4,6},{5,7},{6,4},{7,5},{8,10},{9,11},{10,... | collective-permute-start | bytes 700424 | tf_op jit(solution)/shard_map/ppermute | solution.py:24
  8.4 4.5 %collective-permute-done.2.refs_0_ = bf16[16,7296]{1,0:T(8,128)(2,1)S(1)} collective-permute-done((bf16[16,7296]{1,0:T(8,128)(2,1)}, bf16[16,7296]{1,0:T(8,128)(2,1)S(1)}, u32[]{:S(2)}, u32[]{:S(2)}) %collective-permute-start.2) | collective-permute-done | bytes 233504 | tf_op jit(solution)/shard_map/ppermute | solution.py:24
  12.9 1.5 %collective-permute-start.4 = (bf16[16,7296]{1,0:T(8,128)(2,1)S(1)}, bf16[16,7296]{1,0:T(8,128)(2,1)S(1)}, u32[]{:S(2)}, u32[]{:S(2)}) collective-permute-start(bf16[16,7296]{1,0:T(8,128)(2,1)S(1)} %collective-permute-done.2.refs_0_), channel_id=1, source_target_pairs={{0,2},{1,3},{2,0},{3,1},{4,6},{5,7},{6,4},{7,5},{8,10},{9,11},{10,... | collective-permute-start | bytes 700424 | tf_op jit(solution)/shard_map/ppermute | solution.py:24
  14.4 4.6 %collective-permute-start.11 = (bf16[16,7296]{1,0:T(8,128)(2,1)}, bf16[16,7296]{1,0:T(8,128)(2,1)S(1)}, u32[]{:S(2)}, u32[]{:S(2)}) collective-permute-start(bf16[16,7296]{1,0:T(8,128)(2,1)} %pack.1.refs_4_), channel_id=1, source_target_pairs={{0,4},{1,5},{2,6},{3,7},{4,0},{5,1},{6,2},{7,3},{8,12},{9,13},{10,... | collective-permute-start | bytes 700424 | tf_op jit(solution)/shard_map/ppermute | solution.py:24
  19.0 0.5 collective-permute-start.3
  20.0 3.9 %collective-permute-done.11.refs_4_ = bf16[16,7296]{1,0:T(8,128)(2,1)S(1)} collective-permute-done((bf16[16,7296]{1,0:T(8,128)(2,1)}, bf16[16,7296]{1,0:T(8,128)(2,1)S(1)}, u32[]{:S(2)}, u32[]{:S(2)}) %collective-permute-start.11) | collective-permute-done | bytes 233504 | tf_op jit(solution)/shard_map/ppermute | solution.py:24
  23.9 2.6 %collective-permute-start = (bf16[16,7296]{1,0:T(8,128)(2,1)}, bf16[16,7296]{1,0:T(8,128)(2,1)S(1)}, u32[]{:S(2)}, u32[]{:S(2)}) collective-permute-start(bf16[16,7296]{1,0:T(8,128)(2,1)} %pack.1.refs_4_), channel_id=1, source_target_pairs={{0,8},{1,9},{2,10},{3,11},{4,12},{5,13},{6,14},{7,15},{8,0},{9,1},... | collective-permute-start | bytes 700424 | tf_op jit(solution)/shard_map/ppermute | solution.py:24
  26.5 0.5 collective-permute-start.13
  27.0 0.9 %copy-done = bf16[16,7296]{1,0:T(8,128)(2,1)S(1)} copy-done((bf16[16,7296]{1,0:T(8,128)(2,1)S(1)}, bf16[16,7296]{1,0:T(8,128)(2,1)}, u32[]{:S(2)}) %copy-start) | copy-done | bytes 233496
  28.0 8.4 %early.1 = (bf16[64,7168]{1,0:T(8,128)(2,1)S(1)}, bf16[128,64]{1,0:T(8,128)(2,1)S(1)}, bf16[8,1024,1024]{2,1,0:T(8,128)(2,1)S(1)}) custom-call(s32[1]{0:T(128)} %bitcast.expert_ref, bf16[16,7296]{1,0:T(8,128)(2,1)S(1)} %collective-permute-done.2.refs_0_, bf16[16,7296]{1,0:T(8,128)(2,1)S(1)} %collective-permute-done.3.refs_1_, ...), custom_call_target="tpu_custom_call" | custom-call | flops 117440512 | bytes 16777216 | tf_op jit(solution)/shard_map/early/pallas_call | solution.py:129
  36.6 1.5 %collective-permute-start.9 = (bf16[16,7296]{1,0:T(8,128)(2,1)S(1)}, bf16[16,7296]{1,0:T(8,128)(2,1)S(1)}, u32[]{:S(2)}, u32[]{:S(2)}) collective-permute-start(bf16[16,7296]{1,0:T(8,128)(2,1)S(1)} %collective-permute-done.refs_0_), channel_id=1, source_target_pairs={{0,2},{1,3},{2,0},{3,1},{4,6},{5,7},{6,4},{7,5},{8,10},{9,11},{10,... | collective-permute-start | bytes 700424 | tf_op jit(solution)/shard_map/ppermute | solution.py:24
  38.2 0.5 collective-permute-start.1
  38.7 4.9 %collective-permute-done.9.refs_2_ = bf16[16,7296]{1,0:T(8,128)(2,1)S(1)} collective-permute-done((bf16[16,7296]{1,0:T(8,128)(2,1)S(1)}, bf16[16,7296]{1,0:T(8,128)(2,1)S(1)}, u32[]{:S(2)}, u32[]{:S(2)}) %collective-permute-start.9) | collective-permute-done | bytes 233504 | tf_op jit(solution)/shard_map/ppermute | solution.py:24
  43.5 1.5 %collective-permute-done.10.refs_3_ = bf16[16,7296]{1,0:T(8,128)(2,1)S(1)} collective-permute-done((bf16[16,7296]{1,0:T(8,128)(2,1)S(1)}, bf16[16,7296]{1,0:T(8,128)(2,1)S(1)}, u32[]{:S(2)}, u32[]{:S(2)}) %collective-permute-start.10) | collective-permute-done | bytes 233504 | tf_op jit(solution)/shard_map/ppermute | solution.py:24
  45.0 13.0 %expert.1 = (bf16[16,7168]{1,0:T(8,128)(2,1)S(1)}, bf16[16,7168]{1,0:T(8,128)(2,1)S(1)}, bf16[16,7168]{1,0:T(8,128)(2,1)S(1)}, bf16[16,7168]{1,0:T(8,128)(2,1)S(...) custom-call(s32[1]{0:T(128)} %bitcast.expert_ref, ...), custom_call_target="tpu_custom_call" | custom-call | flops 5637144576 | bytes 44040192 | tf_op jit(solution)/shard_map/expert/pallas_call | solution.py:216
  58.2 0.4 collective-permute-start.23
  58.7 0.8 collective-permute-done.18.refs_1_
  59.6 1.4 %collective-permute-start.19 = (bf16[16,7168]{1,0:T(8,128)(2,1)S(1)}, bf16[16,7168]{1,0:T(8,128)(2,1)S(1)}, u32[]{:S(2)}, u32[]{:S(2)}) collective-permute-start(bf16[16,7168]{1,0:T(8,128)(2,1)S(1)} %add.10), channel_id=1, source_target_pairs={{0,2},{1,3},{2,0},{3,1},{4,6},{5,7},{6,4},{7,5},{8,10},{9,11},{10,... | collective-permute-start | bytes 688136 | tf_op jit(solution)/shard_map/ppermute | solution.py:24
  61.1 0.5 collective-permute-start.22
  61.6 0.7 collective-permute-start.24
  62.3 5.8 %collective-permute-done.19.refs_2_ = bf16[16,7168]{1,0:T(8,128)(2,1)S(1)} collective-permute-done((bf16[16,7168]{1,0:T(8,128)(2,1)S(1)}, bf16[16,7168]{1,0:T(8,128)(2,1)S(1)}, u32[]{:S(2)}, u32[]{:S(2)}) %collective-permute-start.19) | collective-permute-done | bytes 229408 | tf_op jit(solution)/shard_map/ppermute | solution.py:24
  68.2 1.6 %collective-permute-start.20 = (bf16[16,7168]{1,0:T(8,128)(2,1)S(1)}, bf16[16,7168]{1,0:T(8,128)(2,1)S(1)}, u32[]{:S(2)}, u32[]{:S(2)}) collective-permute-start(bf16[16,7168]{1,0:T(8,128)(2,1)S(1)} %add.11), channel_id=1, source_target_pairs={{0,12},{1,13},{2,14},{3,15},{4,8},{5,9},{6,10},{7,11},{8,4},{9,5},... | collective-permute-start | bytes 688136 | tf_op jit(solution)/shard_map/ppermute | solution.py:24
  69.9 0.7 collective-permute-start.28
  70.7 1.6 %collective-permute-done.24.refs_2_ = bf16[16,7168]{1,0:T(8,128)(2,1)S(1)} collective-permute-done((bf16[16,7168]{1,0:T(8,128)(2,1)S(1)}, bf16[16,7168]{1,0:T(8,128)(2,1)S(1)}, u32[]{:S(2)}, u32[]{:S(2)}) %collective-permute-start.24) | collective-permute-done | bytes 229408 | tf_op jit(solution)/shard_map/ppermute | solution.py:24
  72.4 4.5 %collective-permute-done.20.refs_2_.refs_1_ = bf16[16,7168]{1,0:T(8,128)(2,1)S(1)} collective-permute-done((bf16[16,7168]{1,0:T(8,128)(2,1)S(1)}, bf16[16,7168]{1,0:T(8,128)(2,1)S(1)}, u32[]{:S(2)}, u32[]{:S(2)}) %collective-permute-start.20) | collective-permute-done | bytes 229408 | tf_op jit(solution)/shard_map/ppermute | solution.py:24
  77.0 1.5 %collective-permute-start.21 = (bf16[16,7168]{1,0:T(8,128)(2,1)S(1)}, bf16[16,7168]{1,0:T(8,128)(2,1)S(1)}, u32[]{:S(2)}, u32[]{:S(2)}) collective-permute-start(bf16[16,7168]{1,0:T(8,128)(2,1)S(1)} %add.12), channel_id=1, source_target_pairs={{0,2},{1,3},{2,0},{3,1},{4,6},{5,7},{6,4},{7,5},{8,10},{9,11},{10,... | collective-permute-start | bytes 688136 | tf_op jit(solution)/shard_map/ppermute | solution.py:24
  78.6 2.6 %collective-permute-start.29 = (bf16[16,7168]{1,0:T(8,128)(2,1)S(1)}, bf16[16,7168]{1,0:T(8,128)(2,1)S(1)}, u32[]{:S(2)}, u32[]{:S(2)}) collective-permute-start(bf16[16,7168]{1,0:T(8,128)(2,1)S(1)} %add.17), channel_id=1, source_target_pairs={{0,8},{1,9},{2,10},{3,11},{4,12},{5,13},{6,14},{7,15},{8,0},{9,1},... | collective-permute-start | bytes 688136 | tf_op jit(solution)/shard_map/ppermute | solution.py:24
  81.2 1.9 %collective-permute-done.21.refs_2_ = bf16[16,7168]{1,0:T(8,128)(2,1)S(1)} collective-permute-done((bf16[16,7168]{1,0:T(8,128)(2,1)S(1)}, bf16[16,7168]{1,0:T(8,128)(2,1)S(1)}, u32[]{:S(2)}, u32[]{:S(2)}) %collective-permute-start.21) | collective-permute-done | bytes 229408 | tf_op jit(solution)/shard_map/ppermute | solution.py:24
  83.2 7.7 %collective-permute-done.29.refs_3_ = bf16[16,7168]{1,0:T(8,128)(2,1)S(1)} collective-permute-done((bf16[16,7168]{1,0:T(8,128)(2,1)S(1)}, bf16[16,7168]{1,0:T(8,128)(2,1)S(1)}, u32[]{:S(2)}, u32[]{:S(2)}) %collective-permute-start.29) | collective-permute-done | bytes 229408 | tf_op jit(solution)/shard_map/ppermute | solution.py:24
  90.9 0.8 add.18
  (42 shorter events, 1.9 us)
Async XLA Ops:
  1.8 11.1 %collective-permute-start.2 = (bf16[16,7296]{1,0:T(8,128)(2,1)}, bf16[16,7296]{1,0:T(8,128)(2,1)S(1)}, u32[]{:S(2)}, u32[]{:S(2)}) collective-permute-start(bf16[16,7296]{1,0:T(8,128)(2,1)} %pack.1.refs_4_), channel_id=1, source_target_pairs={{0,12},{1,13},{2,14},{3,15},{4,8},{5,9},{6,10},{7,11},{8,4},{9,5},... | collective-permute-start | bytes 700424 | tf_op jit(solution)/shard_map/ppermute | solution.py:24
  6.9 12.7 %collective-permute-start.7 = (bf16[16,7296]{1,0:T(8,128)(2,1)}, bf16[16,7296]{1,0:T(8,128)(2,1)S(1)}, u32[]{:S(2)}, u32[]{:S(2)}) collective-permute-start(bf16[16,7296]{1,0:T(8,128)(2,1)} %pack.1.refs_4_), channel_id=1, source_target_pairs={{0,2},{1,3},{2,0},{3,1},{4,6},{5,7},{6,4},{7,5},{8,10},{9,11},{10,... | collective-permute-start | bytes 700424 | tf_op jit(solution)/shard_map/ppermute | solution.py:24
  12.9 6.8 %collective-permute-start.4 = (bf16[16,7296]{1,0:T(8,128)(2,1)S(1)}, bf16[16,7296]{1,0:T(8,128)(2,1)S(1)}, u32[]{:S(2)}, u32[]{:S(2)}) collective-permute-start(bf16[16,7296]{1,0:T(8,128)(2,1)S(1)} %collective-permute-done.2.refs_0_), channel_id=1, source_target_pairs={{0,2},{1,3},{2,0},{3,1},{4,6},{5,7},{6,4},{7,5},{8,10},{9,11},{10,... | collective-permute-start | bytes 700424 | tf_op jit(solution)/shard_map/ppermute | solution.py:24
  14.4 9.5 %collective-permute-start.11 = (bf16[16,7296]{1,0:T(8,128)(2,1)}, bf16[16,7296]{1,0:T(8,128)(2,1)S(1)}, u32[]{:S(2)}, u32[]{:S(2)}) collective-permute-start(bf16[16,7296]{1,0:T(8,128)(2,1)} %pack.1.refs_4_), channel_id=1, source_target_pairs={{0,4},{1,5},{2,6},{3,7},{4,0},{5,1},{6,2},{7,3},{8,12},{9,13},{10,... | collective-permute-start | bytes 700424 | tf_op jit(solution)/shard_map/ppermute | solution.py:24
  19.0 7.5 %collective-permute-start.6 = (bf16[16,7296]{1,0:T(8,128)(2,1)}, bf16[16,7296]{1,0:T(8,128)(2,1)S(1)}, u32[]{:S(2)}, u32[]{:S(2)}) collective-permute-start(bf16[16,7296]{1,0:T(8,128)(2,1)} %pack.1.refs_4_), channel_id=1, source_target_pairs={{0,1},{1,0},{2,3},{3,2},{4,5},{5,4},{6,7},{7,6},{8,9},{9,8},{10,11... | collective-permute-start | bytes 700424 | tf_op jit(solution)/shard_map/ppermute | solution.py:24
  19.0 8.0 %collective-permute-start.3 = (bf16[16,7296]{1,0:T(8,128)(2,1)S(1)}, bf16[16,7296]{1,0:T(8,128)(2,1)S(1)}, u32[]{:S(2)}, u32[]{:S(2)}) collective-permute-start(bf16[16,7296]{1,0:T(8,128)(2,1)S(1)} %collective-permute-done.2.refs_0_), channel_id=1, source_target_pairs={{0,1},{1,0},{2,3},{3,2},{4,5},{5,4},{6,7},{7,6},{8,9},{9,8},{10,11... | collective-permute-start | bytes 700424 | tf_op jit(solution)/shard_map/ppermute | solution.py:24
  19.5 7.5 %collective-permute-start.8 = (bf16[16,7296]{1,0:T(8,128)(2,1)S(1)}, bf16[16,7296]{1,0:T(8,128)(2,1)S(1)}, u32[]{:S(2)}, u32[]{:S(2)}) collective-permute-start(bf16[16,7296]{1,0:T(8,128)(2,1)S(1)} %collective-permute-done.7.refs_6_), channel_id=1, source_target_pairs={{0,1},{1,0},{2,3},{3,2},{4,5},{5,4},{6,7},{7,6},{8,9},{9,8},{10,11... | collective-permute-start | bytes 700424 | tf_op jit(solution)/shard_map/ppermute | solution.py:24
  19.7 7.3 %collective-permute-start.5 = (bf16[16,7296]{1,0:T(8,128)(2,1)S(1)}, bf16[16,7296]{1,0:T(8,128)(2,1)S(1)}, u32[]{:S(2)}, u32[]{:S(2)}) collective-permute-start(bf16[16,7296]{1,0:T(8,128)(2,1)S(1)} %collective-permute-done.4.refs_2_), channel_id=1, source_target_pairs={{0,1},{1,0},{2,3},{3,2},{4,5},{5,4},{6,7},{7,6},{8,9},{9,8},{10,11... | collective-permute-start | bytes 700424 | tf_op jit(solution)/shard_map/ppermute | solution.py:24
  23.9 12.7 %collective-permute-start = (bf16[16,7296]{1,0:T(8,128)(2,1)}, bf16[16,7296]{1,0:T(8,128)(2,1)S(1)}, u32[]{:S(2)}, u32[]{:S(2)}) collective-permute-start(bf16[16,7296]{1,0:T(8,128)(2,1)} %pack.1.refs_4_), channel_id=1, source_target_pairs={{0,8},{1,9},{2,10},{3,11},{4,12},{5,13},{6,14},{7,15},{8,0},{9,1},... | collective-permute-start | bytes 700424 | tf_op jit(solution)/shard_map/ppermute | solution.py:24
  26.5 12.2 %collective-permute-start.13 = (bf16[16,7296]{1,0:T(8,128)(2,1)S(1)}, bf16[16,7296]{1,0:T(8,128)(2,1)S(1)}, u32[]{:S(2)}, u32[]{:S(2)}) collective-permute-start(bf16[16,7296]{1,0:T(8,128)(2,1)S(1)} %collective-permute-done.11.refs_4_), channel_id=1, source_target_pairs={{0,2},{1,3},{2,0},{3,1},{4,6},{5,7},{6,4},{7,5},{8,10},{9,11},{10,... | collective-permute-start | bytes 700424 | tf_op jit(solution)/shard_map/ppermute | solution.py:24
  27.0 0.9 %copy-start = (bf16[16,7296]{1,0:T(8,128)(2,1)S(1)}, bf16[16,7296]{1,0:T(8,128)(2,1)}, u32[]{:S(2)}) copy-start(bf16[16,7296]{1,0:T(8,128)(2,1)} %pack.1.refs_4_) | copy-start | bytes 700420
  36.6 6.9 %collective-permute-start.9 = (bf16[16,7296]{1,0:T(8,128)(2,1)S(1)}, bf16[16,7296]{1,0:T(8,128)(2,1)S(1)}, u32[]{:S(2)}, u32[]{:S(2)}) collective-permute-start(bf16[16,7296]{1,0:T(8,128)(2,1)S(1)} %collective-permute-done.refs_0_), channel_id=1, source_target_pairs={{0,2},{1,3},{2,0},{3,1},{4,6},{5,7},{6,4},{7,5},{8,10},{9,11},{10,... | collective-permute-start | bytes 700424 | tf_op jit(solution)/shard_map/ppermute | solution.py:24
  38.1 5.4 %collective-permute-start.12 = (bf16[16,7296]{1,0:T(8,128)(2,1)S(1)}, bf16[16,7296]{1,0:T(8,128)(2,1)S(1)}, u32[]{:S(2)}, u32[]{:S(2)}) collective-permute-start(bf16[16,7296]{1,0:T(8,128)(2,1)S(1)} %collective-permute-done.11.refs_4_), channel_id=1, source_target_pairs={{0,1},{1,0},{2,3},{3,2},{4,5},{5,4},{6,7},{7,6},{8,9},{9,8},{10,11... | collective-permute-start | bytes 700424 | tf_op jit(solution)/shard_map/ppermute | solution.py:24
  38.2 5.4 %collective-permute-start.1 = (bf16[16,7296]{1,0:T(8,128)(2,1)S(1)}, bf16[16,7296]{1,0:T(8,128)(2,1)S(1)}, u32[]{:S(2)}, u32[]{:S(2)}) collective-permute-start(bf16[16,7296]{1,0:T(8,128)(2,1)S(1)} %collective-permute-done.refs_0_), channel_id=1, source_target_pairs={{0,1},{1,0},{2,3},{3,2},{4,5},{5,4},{6,7},{7,6},{8,9},{9,8},{10,11... | collective-permute-start | bytes 700424 | tf_op jit(solution)/shard_map/ppermute | solution.py:24
  38.7 4.9 %collective-permute-start.14 = (bf16[16,7296]{1,0:T(8,128)(2,1)S(1)}, bf16[16,7296]{1,0:T(8,128)(2,1)S(1)}, u32[]{:S(2)}, u32[]{:S(2)}) collective-permute-start(bf16[16,7296]{1,0:T(8,128)(2,1)S(1)} %collective-permute-done.13.refs_6_), channel_id=1, source_target_pairs={{0,1},{1,0},{2,3},{3,2},{4,5},{5,4},{6,7},{7,6},{8,9},{9,8},{10,11... | collective-permute-start | bytes 700424 | tf_op jit(solution)/shard_map/ppermute | solution.py:24
  43.5 1.5 %collective-permute-start.10 = (bf16[16,7296]{1,0:T(8,128)(2,1)S(1)}, bf16[16,7296]{1,0:T(8,128)(2,1)S(1)}, u32[]{:S(2)}, u32[]{:S(2)}) collective-permute-start(bf16[16,7296]{1,0:T(8,128)(2,1)S(1)} %collective-permute-done.9.refs_2_), channel_id=1, source_target_pairs={{0,1},{1,0},{2,3},{3,2},{4,5},{5,4},{6,7},{7,6},{8,9},{9,8},{10,11... | collective-permute-start | bytes 700424 | tf_op jit(solution)/shard_map/ppermute | solution.py:24
  58.0 1.6 %collective-permute-start.18 = (bf16[16,7168]{1,0:T(8,128)(2,1)S(1)}, bf16[16,7168]{1,0:T(8,128)(2,1)S(1)}, u32[]{:S(2)}, u32[]{:S(2)}) collective-permute-start(bf16[16,7168]{1,0:T(8,128)(2,1)S(1)} %get-tuple-element.38), channel_id=1, source_target_pairs={{0,1},{1,0},{2,3},{3,2},{4,5},{5,4},{6,7},{7,6},{8,9},{9,8},{10,11... | collective-permute-start | bytes 688136 | tf_op jit(solution)/shard_map/ppermute | solution.py:24
  58.2 3.4 %collective-permute-start.23 = (bf16[16,7168]{1,0:T(8,128)(2,1)S(1)}, bf16[16,7168]{1,0:T(8,128)(2,1)S(1)}, u32[]{:S(2)}, u32[]{:S(2)}) collective-permute-start(bf16[16,7168]{1,0:T(8,128)(2,1)S(1)} %get-tuple-element.42), channel_id=1, source_target_pairs={{0,1},{1,0},{2,3},{3,2},{4,5},{5,4},{6,7},{7,6},{8,9},{9,8},{10,11... | collective-permute-start | bytes 688136 | tf_op jit(solution)/shard_map/ppermute | solution.py:24
  58.6 3.8 %collective-permute-start.17 = (bf16[16,7168]{1,0:T(8,128)(2,1)S(1)}, bf16[16,7168]{1,0:T(8,128)(2,1)S(1)}, u32[]{:S(2)}, u32[]{:S(2)}) collective-permute-start(bf16[16,7168]{1,0:T(8,128)(2,1)S(1)} %get-tuple-element.36), channel_id=1, source_target_pairs={{0,1},{1,0},{2,3},{3,2},{4,5},{5,4},{6,7},{7,6},{8,9},{9,8},{10,11... | collective-permute-start | bytes 688136 | tf_op jit(solution)/shard_map/ppermute | solution.py:24
  59.6 8.5 %collective-permute-start.19 = (bf16[16,7168]{1,0:T(8,128)(2,1)S(1)}, bf16[16,7168]{1,0:T(8,128)(2,1)S(1)}, u32[]{:S(2)}, u32[]{:S(2)}) collective-permute-start(bf16[16,7168]{1,0:T(8,128)(2,1)S(1)} %add.10), channel_id=1, source_target_pairs={{0,2},{1,3},{2,0},{3,1},{4,6},{5,7},{6,4},{7,5},{8,10},{9,11},{10,... | collective-permute-start | bytes 688136 | tf_op jit(solution)/shard_map/ppermute | solution.py:24
  61.1 8.8 %collective-permute-start.27 = (bf16[16,7168]{1,0:T(8,128)(2,1)S(1)}, bf16[16,7168]{1,0:T(8,128)(2,1)S(1)}, u32[]{:S(2)}, u32[]{:S(2)}) collective-permute-start(bf16[16,7168]{1,0:T(8,128)(2,1)S(1)} %get-tuple-element.46), channel_id=1, source_target_pairs={{0,1},{1,0},{2,3},{3,2},{4,5},{5,4},{6,7},{7,6},{8,9},{9,8},{10,11... | collective-permute-start | bytes 688136 | tf_op jit(solution)/shard_map/ppermute | solution.py:24
  61.1 8.8 %collective-permute-start.22 = (bf16[16,7168]{1,0:T(8,128)(2,1)S(1)}, bf16[16,7168]{1,0:T(8,128)(2,1)S(1)}, u32[]{:S(2)}, u32[]{:S(2)}) collective-permute-start(bf16[16,7168]{1,0:T(8,128)(2,1)S(1)} %get-tuple-element.40), channel_id=1, source_target_pairs={{0,1},{1,0},{2,3},{3,2},{4,5},{5,4},{6,7},{7,6},{8,9},{9,8},{10,11... | collective-permute-start | bytes 688136 | tf_op jit(solution)/shard_map/ppermute | solution.py:24
  61.6 10.6 %collective-permute-start.24 = (bf16[16,7168]{1,0:T(8,128)(2,1)S(1)}, bf16[16,7168]{1,0:T(8,128)(2,1)S(1)}, u32[]{:S(2)}, u32[]{:S(2)}) collective-permute-start(bf16[16,7168]{1,0:T(8,128)(2,1)S(1)} %add.14), channel_id=1, source_target_pairs={{0,2},{1,3},{2,0},{3,1},{4,6},{5,7},{6,4},{7,5},{8,10},{9,11},{10,... | collective-permute-start | bytes 688136 | tf_op jit(solution)/shard_map/ppermute | solution.py:24
  62.3 10.0 %collective-permute-start.16 = (bf16[16,7168]{1,0:T(8,128)(2,1)S(1)}, bf16[16,7168]{1,0:T(8,128)(2,1)S(1)}, u32[]{:S(2)}, u32[]{:S(2)}) collective-permute-start(bf16[16,7168]{1,0:T(8,128)(2,1)S(1)} %get-tuple-element.34), channel_id=1, source_target_pairs={{0,1},{1,0},{2,3},{3,2},{4,5},{5,4},{6,7},{7,6},{8,9},{9,8},{10,11... | collective-permute-start | bytes 688136 | tf_op jit(solution)/shard_map/ppermute | solution.py:24
  68.2 8.7 %collective-permute-start.20 = (bf16[16,7168]{1,0:T(8,128)(2,1)S(1)}, bf16[16,7168]{1,0:T(8,128)(2,1)S(1)}, u32[]{:S(2)}, u32[]{:S(2)}) collective-permute-start(bf16[16,7168]{1,0:T(8,128)(2,1)S(1)} %add.11), channel_id=1, source_target_pairs={{0,12},{1,13},{2,14},{3,15},{4,8},{5,9},{6,10},{7,11},{8,4},{9,5},... | collective-permute-start | bytes 688136 | tf_op jit(solution)/shard_map/ppermute | solution.py:24
  69.8 8.7 %collective-permute-start.26 = (bf16[16,7168]{1,0:T(8,128)(2,1)S(1)}, bf16[16,7168]{1,0:T(8,128)(2,1)S(1)}, u32[]{:S(2)}, u32[]{:S(2)}) collective-permute-start(bf16[16,7168]{1,0:T(8,128)(2,1)S(1)} %get-tuple-element.44), channel_id=1, source_target_pairs={{0,1},{1,0},{2,3},{3,2},{4,5},{5,4},{6,7},{7,6},{8,9},{9,8},{10,11... | collective-permute-start | bytes 688136 | tf_op jit(solution)/shard_map/ppermute | solution.py:24
  69.9 8.6 %collective-permute-start.28 = (bf16[16,7168]{1,0:T(8,128)(2,1)S(1)}, bf16[16,7168]{1,0:T(8,128)(2,1)S(1)}, u32[]{:S(2)}, u32[]{:S(2)}) collective-permute-start(bf16[16,7168]{1,0:T(8,128)(2,1)S(1)} %add.16), channel_id=1, source_target_pairs={{0,2},{1,3},{2,0},{3,1},{4,6},{5,7},{6,4},{7,5},{8,10},{9,11},{10,... | collective-permute-start | bytes 688136 | tf_op jit(solution)/shard_map/ppermute | solution.py:24
  72.2 8.9 %collective-permute-start.15 = (bf16[16,7168]{1,0:T(8,128)(2,1)S(1)}, bf16[16,7168]{1,0:T(8,128)(2,1)S(1)}, u32[]{:S(2)}, u32[]{:S(2)}) collective-permute-start(bf16[16,7168]{1,0:T(8,128)(2,1)S(1)} %get-tuple-element.32), channel_id=1, source_target_pairs={{0,1},{1,0},{2,3},{3,2},{4,5},{5,4},{6,7},{7,6},{8,9},{9,8},{10,11... | collective-permute-start | bytes 688136 | tf_op jit(solution)/shard_map/ppermute | solution.py:24
  72.3 10.8 %collective-permute-start.25 = (bf16[16,7168]{1,0:T(8,128)(2,1)S(1)}, bf16[16,7168]{1,0:T(8,128)(2,1)S(1)}, u32[]{:S(2)}, u32[]{:S(2)}) collective-permute-start(bf16[16,7168]{1,0:T(8,128)(2,1)S(1)} %add.15), channel_id=1, source_target_pairs={{0,4},{1,5},{2,6},{3,7},{4,0},{5,1},{6,2},{7,3},{8,12},{9,13},{10,... | collective-permute-start | bytes 688136 | tf_op jit(solution)/shard_map/ppermute | solution.py:24
  77.0 6.1 %collective-permute-start.21 = (bf16[16,7168]{1,0:T(8,128)(2,1)S(1)}, bf16[16,7168]{1,0:T(8,128)(2,1)S(1)}, u32[]{:S(2)}, u32[]{:S(2)}) collective-permute-start(bf16[16,7168]{1,0:T(8,128)(2,1)S(1)} %add.12), channel_id=1, source_target_pairs={{0,2},{1,3},{2,0},{3,1},{4,6},{5,7},{6,4},{7,5},{8,10},{9,11},{10,... | collective-permute-start | bytes 688136 | tf_op jit(solution)/shard_map/ppermute | solution.py:24
  78.6 12.3 %collective-permute-start.29 = (bf16[16,7168]{1,0:T(8,128)(2,1)S(1)}, bf16[16,7168]{1,0:T(8,128)(2,1)S(1)}, u32[]{:S(2)}, u32[]{:S(2)}) collective-permute-start(bf16[16,7168]{1,0:T(8,128)(2,1)S(1)} %add.17), channel_id=1, source_target_pairs={{0,8},{1,9},{2,10},{3,11},{4,12},{5,13},{6,14},{7,15},{8,0},{9,1},... | collective-permute-start | bytes 688136 | tf_op jit(solution)/shard_map/ppermute | solution.py:24
